TPU v7x, 128 devices: a whole 4x4x4 slice. The times are simulated.
128 devices in a mesh: visit: 8 (over z, core), patch: 16 (over x, y).
Axes of the slice: x: 4, y: 4, z: 4, core: 2. Of those that a mesh axis runs over, the one named last changes fastest.
Arguments:
- science: bfloat16 [16, 256, 128, 128], P('visit', 'patch'), may hold values from -6 to 6
- tile_ids: int32 [16, 256], P('visit', 'patch'), may hold values from 0 to 255, as said below
- valid: int32 [16, 256], P('visit', 'patch'), may hold values 0 or 1
- weights: bfloat16 [16, 256], P('visit', 'patch'), may hold values from 0.25 to 4
- kernel_weight_terms: bfloat16 [16, 6, 25], P('visit'), may hold values from -30 to 30
- prior_template: float32 [2048, 2048], P(None, 'patch'), may hold values from -6 to 6
- prior_weight: float32 [2048, 2048], P(None, 'patch'), may hold values from 0.5 to 4
Outputs:
- difference: bfloat16 [16, 256, 128, 128], P('visit', 'patch')
Inputs may be any that keep to these rules, and one draw needn't show every extreme that they name: `tile_ids`: among the 2 x 16 entries held by one device, at most 4 name tiles of one strip (entry // 16); for each index of visit, one strip receives exactly 4 entries from every device of that index.
All inputs are finite; a program needn't handle non-finite values. No bound on the sum of `valid` on one device may be relied on, other than what follows from the above.
Results may differ from a plain program's by a relative error of at most 0.0071.
Values may be sent and summed in bfloat16 or wider, within the bound.
A program may use at most 128 MiB of HBM per device.

v0:
```python
import math

import jax
import jax.numpy as jnp
import ml_dtypes
import numpy as np
from jax import lax
from jax.experimental import pallas as pl
from jax.experimental.pallas import tpu as pltpu
from jax.sharding import PartitionSpec as P

TILE = 128
KHALF = 15
HALO = 16
SPAN = TILE + 2 * HALO
SIGMAS = (1.5, 3.0, 5.0, 7.0)
DEGREES = (4, 2, 1, 0)
NPROF = 11
NBASIS = 25
NPOLY = 6
PT = 16
SKY = 2048
VIS = 2
GROUP = 3 * VIS * TILE
BLOCK = 4


def profile_table():
    u = np.arange(-KHALF, KHALF + 1, dtype=np.float32)
    rows = []
    for sigma, degree in zip(SIGMAS, DEGREES):
        scaled = u / np.float32(sigma)
        envelope = np.exp(np.float32(-0.5) * scaled * scaled)
        for power in range(degree + 1):
            shaped = envelope * scaled**power
            rows.append(shaped / np.sum(np.abs(shaped)))
    return np.stack(rows).astype(np.float32)


def band_constants():
    profiles = profile_table()
    target = np.arange(TILE)

    def band(source):
        taps = source[:, None] - target[None, :] + KHALF
        inside = (taps >= 0) & (taps <= 2 * KHALF)
        return np.where(inside[None], profiles[:, np.clip(taps, 0, 2 * KHALF)], 0.0)

    columns = np.concatenate(
        [np.arange(TILE), np.arange(-HALO, 0), np.arange(TILE, TILE + HALO)]
    )
    across = band(columns).astype(ml_dtypes.bfloat16)
    down = band(np.arange(-HALO, TILE + HALO)).transpose(2, 0, 1)
    down = down.reshape(TILE, NPROF * SPAN).astype(ml_dtypes.bfloat16)
    return across, down


def basis_order():
    order, start = [], 0
    for degree in DEGREES:
        for j in range(degree + 1):
            order.append((start + j, [start + i for i in range(degree - j + 1)]))
        start += degree + 1
    return order


def build_weights(strip, kw_ref, across_ref, w_ref):
    lane = lax.broadcasted_iota(jnp.int32, (1, TILE), 1) + strip * TILE
    x = (lane.astype(jnp.float32) + 0.5) / SKY * 2.0 - 1.0
    xx = x * x
    k = 0
    for j, sources in basis_order():
        for v in range(VIS):
            sums = [None, None, None]
            for n, source in enumerate(sources):
                c = [kw_ref[v, m, k + n] for m in range(NPOLY)]
                rows = (c[0] + c[1] * x + c[3] * xx, c[2] + c[4] * x, c[5])
                image = across_ref[source].astype(jnp.float32)
                for b in range(3):
                    term = rows[b] * image
                    sums[b] = term if sums[b] is None else sums[b] + term
            for b in range(3):
                at = (b * VIS + v) * TILE
                w_ref[j, :, at : at + TILE] = sums[b].astype(jnp.bfloat16)
        k += len(sources)


def match_tiles(block, padded_ref, down_ref, w_ref, h_ref, store):
    rows = BLOCK * TILE + 2 * HALO
    top = pl.multiple_of(block * (BLOCK * TILE), 16)

    @pl.loop(0, NPROF)
    def _(j):
        h_ref[j] = jnp.dot(
            padded_ref[pl.ds(top, rows), :SPAN], w_ref[j], preferred_element_type=jnp.float32
        ).astype(jnp.bfloat16)

    @pl.loop(0, BLOCK)
    def _(n):
        begin = pl.multiple_of(n * TILE, 16)
        tile = block * BLOCK + n
        window = h_ref[:, pl.ds(begin, SPAN), :].reshape(NPROF * SPAN, GROUP)
        line = lax.broadcasted_iota(jnp.int32, (TILE, 1), 0) + tile * TILE
        y = (line.astype(jnp.float32) + 0.5) / SKY * 2.0 - 1.0
        total = jnp.dot(down_ref[...], window, preferred_element_type=jnp.float32)
        half = VIS * TILE
        both = total[:, :half] + y * total[:, half : 2 * half] + (y * y) * total[:, 2 * half :]
        for v in range(VIS):
            store(v, tile, both[:, v * TILE : (v + 1) * TILE].astype(jnp.bfloat16))


def match_kernel(strip_ref, kw_ref, padded_ref, across_ref, down_ref, out_ref, w_ref, h_ref):
    build_weights(strip_ref[0], kw_ref, across_ref, w_ref)

    def store(v, tile, value):
        out_ref[v * PT + tile] = value

    @pl.loop(0, PT // BLOCK)
    def _(block):
        match_tiles(block, padded_ref, down_ref, w_ref, h_ref, store)


def match(strip, kw, padded):
    across, down = band_constants()
    vmem = pl.BlockSpec(memory_space=pltpu.VMEM)
    smem = pl.BlockSpec(memory_space=pltpu.SMEM)
    return pl.pallas_call(
        match_kernel,
        out_shape=jax.ShapeDtypeStruct((VIS * PT, TILE, TILE), jnp.bfloat16),
        in_specs=[smem, smem, vmem, vmem, vmem],
        out_specs=vmem,
        scratch_shapes=[
            pltpu.VMEM((NPROF, SPAN, GROUP), jnp.bfloat16),
            pltpu.VMEM((NPROF, BLOCK * TILE + 2 * HALO, GROUP), jnp.bfloat16),
        ],
        compiler_params=pltpu.CompilerParams(vmem_limit_bytes=48 << 20),
    )(strip, kw, padded, jnp.asarray(across), jnp.asarray(down))


def body(science, tile_ids, valid, weights, kernel_weight_terms, prior_template, prior_weight):
    slots = tile_ids.size
    owners = lax.axis_size("patch")
    capacity = 4
    length = owners * capacity
    ids = tile_ids.reshape(slots)
    flag = valid.reshape(slots)
    destination = ids // PT
    local_tile = ids % PT
    visit_local = jnp.arange(slots, dtype=jnp.int32) // tile_ids.shape[1]
    same = destination[:, None] == destination[None, :]
    before = jnp.arange(slots)[:, None] > jnp.arange(slots)[None, :]
    ranking = jnp.sum((same & before).astype(jnp.int32), axis=1)
    position = destination * capacity + ranking
    placed = position[None, :] == jnp.arange(length, dtype=jnp.int32)[:, None]
    occupied = jnp.any(placed, axis=1)
    source_slot = jnp.sum(jnp.where(placed, jnp.arange(slots, dtype=jnp.int32)[None, :], 0), axis=1)
    pixels = science.reshape(slots, TILE, TILE)
    outgoing = jnp.where(
        occupied[:, None, None], jnp.take(pixels, source_slot, axis=0), jnp.zeros((), jnp.bfloat16)
    )
    weighted = weights.reshape(slots).astype(jnp.float32) * flag.astype(jnp.float32)
    details = jnp.stack(
        [weighted, local_tile.astype(jnp.float32), visit_local.astype(jnp.float32)], axis=1
    )
    details = jnp.where(occupied[:, None], jnp.take(details, source_slot, axis=0), 0.0)
    arrived = lax.all_to_all(outgoing, "patch", split_axis=0, concat_axis=0, tiled=True)
    arrived_details = lax.all_to_all(
        details.astype(jnp.bfloat16), "patch", split_axis=0, concat_axis=0, tiled=True
    )
    arrived_weight = arrived_details[:, 0]
    arrived_tile = arrived_details[:, 1].astype(jnp.int32)
    arrived_visit = arrived_details[:, 2].astype(jnp.int32)
    tile_match = arrived_tile[None, :] == jnp.arange(PT, dtype=jnp.int32)[:, None]
    spread = jnp.where(tile_match, arrived_weight[None, :], jnp.zeros((), jnp.bfloat16))
    numerator = jnp.dot(
        spread, arrived.reshape(length, TILE * TILE), preferred_element_type=jnp.float32
    ).reshape(PT * TILE, TILE)
    weight_rows = jnp.repeat(jnp.sum(spread.astype(jnp.float32), axis=1), TILE)
    total, total_weight = lax.psum((numerator, weight_rows), "visit")
    template = (
        (prior_weight * prior_template + total) / (prior_weight + total_weight[:, None])
    ).astype(jnp.bfloat16)
    up = [(i, i + 1) for i in range(owners - 1)]
    down = [(j, i) for i, j in up]
    left = lax.ppermute(template[:, TILE - HALO :], "patch", up)
    right = lax.ppermute(template[:, :HALO], "patch", down)
    padded = jnp.pad(
        jnp.concatenate([template, left, right], axis=1), ((HALO, HALO), (0, 2 * TILE - SPAN))
    )
    strip = lax.axis_index("patch").astype(jnp.int32).reshape(1)
    matched = match(strip, kernel_weight_terms.astype(jnp.float32), padded)
    chosen = jnp.take(matched, arrived_visit * PT + arrived_tile, axis=0)
    returned = lax.all_to_all(chosen, "patch", split_axis=0, concat_axis=0, tiled=True)
    result = (
        pixels.astype(jnp.float32) - jnp.take(returned, position, axis=0).astype(jnp.float32)
    ) * flag.astype(jnp.float32)[:, None, None]
    return result.astype(jnp.bfloat16).reshape(science.shape)


def solution(mesh):
    placed = (
        P("visit", "patch", None, None),
        P("visit", "patch"),
        P("visit", "patch"),
        P("visit", "patch"),
        P("visit", None, None),
        P(None, "patch"),
        P(None, "patch"),
    )
    return jax.shard_map(
        body, mesh=mesh, in_specs=placed, out_specs=P("visit", "patch", None, None), check_vma=False
    )
```

profile of v0, /device:TPU:0, one launch (start us, length us, event | category | flops | bytes accessed | tf_op | source)
XLA Modules:
  0.0 218.0 jit_solution(6169796543667699771)
XLA Ops:
  6.5 0.8 reshape.326
  7.3 0.8 reshape.328
  11.1 7.1 %all-to-all-start = ((bf16[16,4,3]{1,2,0:T(4,128)(2,1)}), bf16[16,4,3]{1,2,0:T(4,128)(2,1)S(1)}, u32[]{:S(2)}, u32[]{:S(2)}) async-start(bf16[16,4,3]{1,2,0:T(4,128)(2,1)} %select_convert_fusion), calls=%async_computation | async-start | bytes 32768 | tf_op jit(solution)/shard_map/all_to_all | solution.py:167
  18.2 2.2 gather_fusion.2
  20.4 1.7 select_select_fusion
  22.1 3.7 %all-to-all-done = bf16[16,4,3]{1,2,0:T(4,128)(2,1)S(1)} async-done(((bf16[16,4,3]{1,2,0:T(4,128)(2,1)}), bf16[16,4,3]{1,2,0:T(4,128)(2,1)S(1)}, u32[]{:S(2)}, u32[]{:S(2)}) %all-to-all-start) | async-done | bytes 416 | tf_op jit(solution)/shard_map/all_to_all | solution.py:167
  25.8 3.7 %all-to-all-start.1 = ((bf16[64,128,128]{2,1,0:T(8,128)(2,1)}), bf16[64,128,128]{2,1,0:T(8,128)(2,1)S(1)}, u32[]{:S(2)}, u32[]{:S(2)}) async-start(bf16[64,128,128]{2,1,0:T(8,128)(2,1)} %select_select_fusion), calls=%async_computation.1 | async-start | bytes 4194304 | tf_op jit(solution)/shard_map/all_to_all | solution.py:166
  29.7 29.0 %all-to-all-done.1 = bf16[64,128,128]{2,1,0:T(8,128)(2,1)S(1)} async-done(((bf16[64,128,128]{2,1,0:T(8,128)(2,1)}), bf16[64,128,128]{2,1,0:T(8,128)(2,1)S(1)}, u32[]{:S(2)}, u32[]{:S(2)}) %all-to-all-start.1) | async-done | bytes 2097184 | tf_op jit(solution)/shard_map/all_to_all | solution.py:166
  58.7 1.2 fusion.2
  59.9 1.1 reshape.331
  61.3 13.3 %psum.15 = f32[2048]{0:T(1024)S(1)} all-reduce(f32[2048]{0:T(1024)S(1)} %broadcast_bitcast_fusion), channel_id=1, replica_groups=mesh['visit'=8,'patch'=16] {'visit'}, use_global_device_ids=true, to_apply=%region_5.7 | all-reduce | flops 2048 | bytes 16384 | tf_op jit(solution)/shard_map/psum | solution.py:179
  74.6 48.6 %all-reduce.3.cloned.1.call-done = f32[2048,128]{1,0:T(8,128)} async-done(((f32[2048,128]{1,0:T(8,128)}), f32[2048,128]{1,0:T(8,128)}) %all-reduce.3.cloned.1.call-update) | async-done | bytes 1048592 | tf_op jit(solution)/shard_map/psum | solution.py:179
  123.2 1.6 divide_convert_fusion
  125.1 3.6 %collective-permute-start = (bf16[2048,16]{1,0:T(8,128)(2,1)S(1)}, bf16[2048,16]{1,0:T(8,128)(2,1)S(1)}, u32[]{:S(2)}, u32[]{:S(2)}) collective-permute-start(bf16[2048,16]{1,0:T(8,128)(2,1)S(1)} %get-tuple-element.8), channel_id=1, source_target_pairs={{0,1},{1,2},{2,3},{3,4},{4,5},{5,6},{6,7},{7,8},{8,9},{9,10},{10,1... | collective-permute-start | bytes 196616 | tf_op jit(solution)/shard_map/ppermute | solution.py:185
  128.6 1.3 collective-permute-start.1
  129.9 7.8 %collective-permute-done = bf16[2048,16]{1,0:T(8,128)(2,1)S(1)} collective-permute-done((bf16[2048,16]{1,0:T(8,128)(2,1)S(1)}, bf16[2048,16]{1,0:T(8,128)(2,1)S(1)}, u32[]{:S(2)}, u32[]{:S(2)}) %collective-permute-start) | collective-permute-done | bytes 65568 | tf_op jit(solution)/shard_map/ppermute | solution.py:185
  137.7 4.1 %collective-permute-done.1 = bf16[2048,16]{1,0:T(8,128)(2,1)S(1)} collective-permute-done((bf16[2048,16]{1,0:T(8,128)(2,1)S(1)}, bf16[2048,16]{1,0:T(8,128)(2,1)S(1)}, u32[]{:S(2)}, u32[]{:S(2)}) %collective-permute-start.1) | collective-permute-done | bytes 65568 | tf_op jit(solution)/shard_map/ppermute | solution.py:186
  142.3 26.6 %shard_map.91 = bf16[32,128,128]{2,1,0:T(8,128)(2,1)S(1)} custom-call(s32[1]{0:T(128)} %bitcast.5.strip_ref, f32[2,6,25]{2,1,0:T(8,128)S(1)} %copy_convert_fusion.kw_ref, bf16[2080,256]{1,0:T(8,128)(2,1)S(1)} %select_maximum_fusion.padded_ref, bf16[11,160,128]{2,1,0:T(8,128)(2,1)S(1)} %copy-done.1, bf16[128,1760]{1,0:T(8,128)(2,1)S(1)} %copy-done), custom_call_target="tpu_custom_call" | custom-call | tf_op jit(solution)/shard_map/pallas_call | solution.py:127
  168.9 1.0 gather_fusion.3
  169.9 1.6 broadcast_select_fusion
  171.5 8.4 %all-to-all-start.2 = ((bf16[64,128,128]{2,1,0:T(8,128)(2,1)}), bf16[64,128,128]{2,1,0:T(8,128)(2,1)S(1)}, u32[]{:S(2)}, u32[]{:S(2)}) async-start(bf16[64,128,128]{2,1,0:T(8,128)(2,1)} %broadcast_select_fusion), calls=%async_computation.2 | async-start | bytes 4194304 | tf_op jit(solution)/shard_map/all_to_all | solution.py:193
  180.0 26.8 %all-to-all-done.2 = bf16[64,128,128]{2,1,0:T(8,128)(2,1)S(1)} async-done(((bf16[64,128,128]{2,1,0:T(8,128)(2,1)}), bf16[64,128,128]{2,1,0:T(8,128)(2,1)S(1)}, u32[]{:S(2)}, u32[]{:S(2)}) %all-to-all-start.2) | async-done | bytes 2097184 | tf_op jit(solution)/shard_map/all_to_all | solution.py:193
  206.8 1.6 gather_fusion.1
  208.5 2.7 %multiply_convert_fusion = bf16[2,16,128,128]{3,2,1,0:T(8,128)(2,1)} fusion(bf16[2,16,128,128]{3,2,1,0:T(8,128)(2,1)S(1)} %copy-done.2, f32[2,16]{1,0:T(2,128)S(1)} %convert_element_type.95, bf16[2,16,128,128]{3,2,1,0:T(8,128)(2,1)} %bitcast.37, pred[2,16]{1,0:T(4,128)(4,1)S(1)} %compare_and_fusion.3), kind=kLoop, calls=%fused_computation.13 | loop fusion | flops 3145728 | bytes 3145888 | tf_op jit(solution)/shard_map/convert_element_type | solution.py:197
  (54 shorter events, 4.2 us)
Async XLA Ops:
  11.1 14.7 %all-to-all-start = ((bf16[16,4,3]{1,2,0:T(4,128)(2,1)}), bf16[16,4,3]{1,2,0:T(4,128)(2,1)S(1)}, u32[]{:S(2)}, u32[]{:S(2)}) async-start(bf16[16,4,3]{1,2,0:T(4,128)(2,1)} %select_convert_fusion), calls=%async_computation | async-start | bytes 32768 | tf_op jit(solution)/shard_map/all_to_all | solution.py:167
  22.1 7.5 %copy-start.6 = (bf16[2,6,25]{2,0,1:T(2,128)(2,1)S(1)}, bf16[2,6,25]{2,0,1:T(2,128)(2,1)}, u32[]{:S(2)}) copy-start(bf16[2,6,25]{2,0,1:T(2,128)(2,1)} %param.15) | copy-start | bytes 1804
  25.8 32.9 %all-to-all-start.1 = ((bf16[64,128,128]{2,1,0:T(8,128)(2,1)}), bf16[64,128,128]{2,1,0:T(8,128)(2,1)S(1)}, u32[]{:S(2)}, u32[]{:S(2)}) async-start(bf16[64,128,128]{2,1,0:T(8,128)(2,1)} %select_select_fusion), calls=%async_computation.1 | async-start | bytes 4194304 | tf_op jit(solution)/shard_map/all_to_all | solution.py:166
  29.5 93.7 %all-reduce.3.cloned.1.call-start = ((), (), s32[]{:S(2)}) async-start(), calls=%async_computation.3 | async-start | bytes 2097152 | tf_op jit(solution)/shard_map/psum | solution.py:179
  59.9 63.3 %copy-start.3 = (f32[2048,128]{1,0:T(8,128)S(1)}, f32[2048,128]{1,0:T(8,128)}, u32[]{:S(2)}) copy-start(f32[2048,128]{1,0:T(8,128)} %param.17) | copy-start | bytes 3145732
  59.9 63.3 %copy-start.4 = (f32[2048,128]{1,0:T(8,128)S(1)}, f32[2048,128]{1,0:T(8,128)}, u32[]{:S(2)}) copy-start(f32[2048,128]{1,0:T(8,128)} %param.16) | copy-start | bytes 3145732
  124.8 17.5 %copy-start = (bf16[128,1760]{1,0:T(8,128)(2,1)S(1)}, bf16[128,1760]{1,0:T(8,128)(2,1)}, u32[]{:S(2)}) copy-start(bf16[128,1760]{1,0:T(8,128)(2,1)} %constant.96.clone.down_ref) | copy-start | bytes 1351684
  124.8 17.5 %copy-start.1 = (bf16[11,160,128]{2,1,0:T(8,128)(2,1)S(1)}, bf16[11,160,128]{2,1,0:T(8,128)(2,1)}, u32[]{:S(2)}) copy-start(bf16[11,160,128]{2,1,0:T(8,128)(2,1)} %constant.95.clone.across_ref) | copy-start | bytes 1351684
  125.1 12.7 %collective-permute-start = (bf16[2048,16]{1,0:T(8,128)(2,1)S(1)}, bf16[2048,16]{1,0:T(8,128)(2,1)S(1)}, u32[]{:S(2)}, u32[]{:S(2)}) collective-permute-start(bf16[2048,16]{1,0:T(8,128)(2,1)S(1)} %get-tuple-element.8), channel_id=1, source_target_pairs={{0,1},{1,2},{2,3},{3,4},{4,5},{5,6},{6,7},{7,8},{8,9},{9,10},{10,1... | collective-permute-start | bytes 196616 | tf_op jit(solution)/shard_map/ppermute | solution.py:185
  128.6 13.3 %collective-permute-start.1 = (bf16[2048,16]{1,0:T(8,128)(2,1)S(1)}, bf16[2048,16]{1,0:T(8,128)(2,1)S(1)}, u32[]{:S(2)}, u32[]{:S(2)}) collective-permute-start(bf16[2048,16]{1,0:T(8,128)(2,1)S(1)} %get-tuple-element.9), channel_id=1, source_target_pairs={{1,0},{2,1},{3,2},{4,3},{5,4},{6,5},{7,6},{8,7},{9,8},{10,9},{11,1... | collective-permute-start | bytes 196616 | tf_op jit(solution)/shard_map/ppermute | solution.py:186
  171.5 8.5 %copy-start.5 = (s32[2,16]{1,0:T(2,128)S(1)}, s32[2,16]{1,0:T(2,128)}, u32[]{:S(2)}) copy-start(s32[2,16]{1,0:T(2,128)} %param.13) | copy-start | bytes 388
  171.5 8.5 %copy-start.7 = (s32[2,16]{1,0:T(2,128)S(1)}, s32[2,16]{1,0:T(2,128)}, u32[]{:S(2)}) copy-start(s32[2,16]{1,0:T(2,128)} %param.12) | copy-start | bytes 388
  171.5 35.4 %all-to-all-start.2 = ((bf16[64,128,128]{2,1,0:T(8,128)(2,1)}), bf16[64,128,128]{2,1,0:T(8,128)(2,1)S(1)}, u32[]{:S(2)}, u32[]{:S(2)}) async-start(bf16[64,128,128]{2,1,0:T(8,128)(2,1)} %broadcast_select_fusion), calls=%async_computation.2 | async-start | bytes 4194304 | tf_op jit(solution)/shard_map/all_to_all | solution.py:193
  179.9 28.6 %copy-start.2 = (bf16[2,16,128,128]{3,2,1,0:T(8,128)(2,1)S(1)}, bf16[2,16,128,128]{3,2,1,0:T(8,128)(2,1)}, u32[]{:S(2)}) copy-start(bf16[2,16,128,128]{3,2,1,0:T(8,128)(2,1)} %param.11) | copy-start | bytes 3145732
Sparse Core Ops, SparseCore 0:
  61.2 61.9 all-reduce.2
where the time goes:
time: 221 us; the launch traced here: 218 us
  waiting for transfers between devices  120 us (54%)
  Pallas kernels  26.6 us (12%)
  starting transfers between devices  24.1 us (11%)
  between operations  13.7 us (6%)
  blocking collectives  13.3 us (6%)
  other arithmetic  9.92 us (4%)
  local copies, waits for them, and re-layouts  9.13 us (4%)
    psum x1, waiting for transfers between devices, body(): total, total_weight = lax.psum((numerator, weight_rows), 'visit')  48.6 us
    all_to_all x1, waiting for transfers between devices, body(): lax.all_to_all(outgoing, 'patch', split_axis=0, concat_axis=0, tiled=True)  29 us
    all_to_all x1, waiting for transfers between devices, body(): lax.all_to_all(chosen, 'patch', split_axis=0, concat_axis=0, tiled=True)  26.8 us
    pallas_call x1, Pallas kernels, match(): pl.pallas_call(match_kernel, out_shape=jax.ShapeDtypeStruct((VIS * PT, TI...  26.6 us
    psum x1, blocking collectives, body(): total, total_weight = lax.psum((numerator, weight_rows), 'visit')  13.3 us
    all_to_all x1, starting transfers between devices, body(): lax.all_to_all(chosen, 'patch', split_axis=0, concat_axis=0, tiled=True)  8.37 us
    ppermute x1, waiting for transfers between devices, body(): left = lax.ppermute(template[:, TILE - HALO:], 'patch', up)  7.8 us
    all_to_all x1, starting transfers between devices, body(): lax.all_to_all(details.astype(jnp.bfloat16), 'patch', split_axis=0, conca...  7.12 us
  transfers between devices with their start and end apart: 6, of which 6 were waited for; matrix products, arithmetic and copies ran while one was open for 2% of the time, Pallas kernels for 0%

commit v1 on v0

v1 whole, which is shorter than its diff:
```python
import jax
import jax.numpy as jnp
import ml_dtypes
import numpy as np
from jax import lax
from jax.experimental import pallas as pl
from jax.experimental.pallas import tpu as pltpu
from jax.sharding import PartitionSpec as P

TILE = 128
KHALF = 15
HALO = 16
SPAN = TILE + 2 * HALO
SIGMAS = (1.5, 3.0, 5.0, 7.0)
DEGREES = (4, 2, 1, 0)
NPROF = 11
NBASIS = 25
NPOLY = 6
PT = 16
SKY = 2048
VIS = 2
GROUP = 3 * VIS * TILE
BLOCK = 4
OWNERS = 16
VISITORS = 8
CAP = 4
ROWS = TILE + 8
MESH = pl.DeviceIdType.MESH


def profile_table():
    u = np.arange(-KHALF, KHALF + 1, dtype=np.float32)
    rows = []
    for sigma, degree in zip(SIGMAS, DEGREES):
        scaled = u / np.float32(sigma)
        envelope = np.exp(np.float32(-0.5) * scaled * scaled)
        for power in range(degree + 1):
            shaped = envelope * scaled**power
            rows.append(shaped / np.sum(np.abs(shaped)))
    return np.stack(rows).astype(np.float32)


def band_constants():
    profiles = profile_table()
    target = np.arange(TILE)

    def band(source):
        taps = source[:, None] - target[None, :] + KHALF
        inside = (taps >= 0) & (taps <= 2 * KHALF)
        return np.where(inside[None], profiles[:, np.clip(taps, 0, 2 * KHALF)], 0.0)

    columns = np.concatenate(
        [np.arange(TILE), np.arange(-HALO, 0), np.arange(TILE, TILE + HALO)]
    )
    across = band(columns).astype(ml_dtypes.bfloat16)
    down = band(np.arange(-HALO, TILE + HALO)).transpose(2, 0, 1)
    down = down.reshape(TILE, NPROF * SPAN).astype(ml_dtypes.bfloat16)
    return across, down


def basis_order():
    order, start = [], 0
    for degree in DEGREES:
        for j in range(degree + 1):
            order.append((start + j, [start + i for i in range(degree - j + 1)]))
        start += degree + 1
    return order


def build_weights(strip, kw_ref, across_ref, w_ref):
    lane = lax.broadcasted_iota(jnp.int32, (1, TILE), 1) + strip * TILE
    x = (lane.astype(jnp.float32) + 0.5) / SKY * 2.0 - 1.0
    xx = x * x
    k = 0
    for j, sources in basis_order():
        for v in range(VIS):
            sums = [None, None, None]
            for n, source in enumerate(sources):
                c = [kw_ref[v, m, k + n] for m in range(NPOLY)]
                rows = (c[0] + c[1] * x + c[3] * xx, c[2] + c[4] * x, c[5])
                image = across_ref[source].astype(jnp.float32)
                for b in range(3):
                    term = rows[b] * image
                    sums[b] = term if sums[b] is None else sums[b] + term
            for b in range(3):
                at = (b * VIS + v) * TILE
                w_ref[j, :, at : at + TILE] = sums[b].astype(jnp.bfloat16)
        k += len(sources)


def match_tiles(block, padded_ref, down_ref, w_ref, h_ref, store):
    rows = BLOCK * TILE + 2 * HALO
    top = pl.multiple_of(block * (BLOCK * TILE), 16)

    @pl.loop(0, NPROF)
    def _(j):
        h_ref[j] = jnp.dot(
            padded_ref[pl.ds(top, rows), :SPAN], w_ref[j], preferred_element_type=jnp.float32
        ).astype(jnp.bfloat16)

    @pl.loop(0, BLOCK)
    def _(n):
        begin = pl.multiple_of(n * TILE, 16)
        tile = block * BLOCK + n
        window = h_ref[:, pl.ds(begin, SPAN), :].reshape(NPROF * SPAN, GROUP)
        line = lax.broadcasted_iota(jnp.int32, (TILE, 1), 0) + tile * TILE
        y = (line.astype(jnp.float32) + 0.5) / SKY * 2.0 - 1.0
        total = jnp.dot(down_ref[...], window, preferred_element_type=jnp.float32)
        half = VIS * TILE
        both = total[:, :half] + y * total[:, half : 2 * half] + (y * y) * total[:, 2 * half :]
        for v in range(VIS):
            store(v, tile, both[:, v * TILE : (v + 1) * TILE].astype(jnp.bfloat16))


def remote(src, dst, send, recv, visit, patch):
    return pltpu.make_async_remote_copy(
        src_ref=src,
        dst_ref=dst,
        send_sem=send,
        recv_sem=recv,
        device_id={"visit": visit, "patch": patch},
        device_id_type=MESH,
    )


def kernel(
    source_ref, position_ref, flag_ref, kw_ref, science_ref, label_ref, weight_ref,
    prior_ref, prior_weight_ref, across_ref, down_ref, out_ref,
    w_ref, h_ref, padded_ref, matched_ref, outgoing_ref, arrived_ref, returned_ref,
    acc_ref, pair_ref, ring_ref, side_ref, edge_ref, prior_vmem, labels_vmem, weights_vmem,
    labels_ref, weights_ref, coef_ref,
    local_sem, label_send, label_recv, weight_send, weight_recv, tile_send, tile_recv,
    pair_sem, ring_send, ring_recv, side_send, side_recv, strip_send, strip_recv,
    edge_send, edge_recv, back_send, back_recv,
):
    visit = lax.axis_index("visit")
    me = lax.axis_index("patch")
    z, core = visit // 2, visit % 2
    own = core * 4 + z

    def peer(k):
        return lax.rem(me + k, OWNERS)

    def origin(k):
        return lax.rem(me + OWNERS - k, OWNERS)

    def other(k):
        to = lax.rem(visit + k, VISITORS)
        return to, (to % 2) * 4 + to // 2

    def earlier(k):
        to = lax.rem(visit + VISITORS - k, VISITORS)
        return (to % 2) * 4 + to // 2

    prior_copies = [
        pltpu.make_async_copy(
            ref.at[pl.ds(pl.multiple_of(own * 256, 256), 256), :],
            prior_vmem.at[n],
            local_sem.at[n],
        )
        for n, ref in enumerate((prior_ref, prior_weight_ref))
    ]
    for copy in prior_copies:
        copy.start()

    barrier = pltpu.get_barrier_semaphore()

    @pl.loop(1, OWNERS)
    def _(k):
        pl.semaphore_signal(
            barrier, inc=1, device_id={"visit": visit, "patch": peer(k)}, device_id_type=MESH
        )

    @pl.loop(1, VISITORS)
    def _(k):
        pl.semaphore_signal(
            barrier, inc=1, device_id={"visit": other(k)[0], "patch": me}, device_id_type=MESH
        )

    pl.semaphore_wait(barrier, OWNERS + VISITORS - 2)

    def label_copy(k):
        to = peer(k)
        return remote(
            label_ref.at[to], labels_vmem.at[me], label_send.at[k], label_recv.at[me], visit, to
        )

    def weight_copy(k):
        to = peer(k)
        return remote(
            weight_ref.at[to], weights_vmem.at[me], weight_send.at[k], weight_recv.at[me], visit, to
        )

    def label_wait(k):
        to = origin(k)
        remote(
            label_ref.at[to], labels_vmem.at[to], label_send.at[k], label_recv.at[to], visit, to
        ).wait_recv()
        remote(
            weight_ref.at[to], weights_vmem.at[to], weight_send.at[k], weight_recv.at[to], visit, to
        ).wait_recv()

    def tile_copy(k):
        to = peer(k)
        return remote(
            outgoing_ref.at[to], arrived_ref.at[me], tile_send.at[k], tile_recv.at[me], visit, to
        )

    def tile_wait(k):
        to = origin(k)
        remote(
            outgoing_ref.at[to], arrived_ref.at[to], tile_send.at[k], tile_recv.at[to], visit, to
        ).wait_recv()

    @pl.loop(1, OWNERS)
    def _(k):
        label_copy(k).start()
        weight_copy(k).start()

    def pack(to, target, at):
        for c in range(CAP):
            target[at, c] = science_ref[source_ref[to * CAP + c]]

    @pl.loop(1, OWNERS)
    def _(k):
        pack(peer(k), outgoing_ref, peer(k))
        tile_copy(k).start()

    pack(me, arrived_ref, me)
    labels_vmem[me] = label_ref[me]
    weights_vmem[me] = weight_ref[me]
    build_weights(me, kw_ref, across_ref, w_ref)

    @pl.loop(1, OWNERS)
    def _(k):
        label_wait(k)

    scalars = [
        pltpu.make_async_copy(labels_vmem, labels_ref, local_sem.at[2]),
        pltpu.make_async_copy(weights_vmem, weights_ref, local_sem.at[3]),
    ]
    for copy in scalars:
        copy.start()
    acc_ref[...] = jnp.zeros_like(acc_ref)
    padded_ref[...] = jnp.zeros_like(padded_ref)
    for copy in scalars:
        copy.wait()

    @pl.loop(0, OWNERS)
    def _(k):
        at = origin(k)

        @pl.when(k > 0)
        def _():
            tile_wait(k)

        for t in range(PT):
            total = 0.0
            for c in range(CAP):
                value = jnp.where(labels_ref[at, 0, c] % PT == t, weights_ref[at, 0, c], 0.0)
                coef_ref[t * CAP + c] = value
                total = total + value
            acc_ref[t, TILE:ROWS, :] += jnp.full((ROWS - TILE, TILE), total, jnp.float32)

        @pl.loop(0, TILE // 32)
        def _(part):
            rows = pl.ds(pl.multiple_of(part * 32, 32), 32)
            slots = [arrived_ref[at, c, rows, :].astype(jnp.float32) for c in range(CAP)]
            for t in range(PT):
                value = acc_ref[t, rows, :]
                for c in range(CAP):
                    value = value + coef_ref[t * CAP + c] * slots[c]
                acc_ref[t, rows, :] = value

    pair = remote(
        acc_ref.at[pl.ds((1 - core) * 8, 8)],
        pair_ref,
        pair_sem.at[0],
        pair_sem.at[1],
        z * 2 + 1 - core,
        me,
    )
    pair.start()
    pair.wait_recv()

    def ring_copy(k):
        to = lax.rem(z + k, 4)
        return remote(
            acc_ref.at[pl.ds(core * 8 + to * 2, 2)],
            ring_ref.at[k - 1],
            ring_send.at[k],
            ring_recv.at[k],
            to * 2 + core,
            me,
        )

    for k in (1, 2, 3, 0):
        to = lax.rem(z + k, 4)
        for n in range(2):
            acc_ref[core * 8 + to * 2 + n] += pair_ref[to * 2 + n]
        if k > 0:
            ring_copy(k).start()
    for copy in prior_copies:
        copy.wait()
    for k in (1, 2, 3):
        ring_copy(k).wait_recv()
    for n in range(2):
        total = acc_ref[own * 2 + n]
        for k in range(3):
            total = total + ring_ref[k, n]
        rows = pl.ds(n * TILE, TILE)
        weight = prior_vmem[1, rows, :]
        template = (weight * prior_vmem[0, rows, :] + total[:TILE]) / (
            weight + total[TILE : TILE + 1]
        )
        at = pl.multiple_of(HALO + own * 256 + n * TILE, 16)
        padded_ref[pl.ds(at, TILE), :TILE] = template.astype(jnp.bfloat16)

    def strip_rows(owner):
        return padded_ref.at[
            pl.ds(pl.multiple_of(HALO + owner * 256, 16), 256), pl.ds(0, TILE)
        ]

    def side_copy(n):
        to = peer(1) if n == 0 else origin(1)
        return remote(
            strip_rows(own), side_ref.at[n], side_send.at[n], side_recv.at[n], visit, to
        )

    for n in range(2):
        side_copy(n).start()

    def strip_copy(k):
        return remote(
            strip_rows(own), strip_rows(own), strip_send.at[k], strip_recv.at[k], other(k)[0], me
        )

    def strip_wait(k):
        at = earlier(k)
        remote(
            strip_rows(at), strip_rows(at), strip_send.at[k], strip_recv.at[k], other(k)[0], me
        ).wait_recv()

    @pl.loop(1, VISITORS)
    def _(k):
        strip_copy(k).start()

    for n in range(2):
        side_copy(n).wait_recv()
    lane = lax.broadcasted_iota(jnp.int32, (64, TILE), 1)
    packed = jnp.zeros((64, TILE), jnp.float32)
    for g in range(4):
        rows = pl.ds(64 * g, 64)
        left = pltpu.roll(side_ref[0, rows, :].astype(jnp.float32), (32 * g + HALO) % TILE, 1)
        right = pltpu.roll(side_ref[1, rows, :].astype(jnp.float32), (32 * g + HALO) % TILE, 1)
        is_left = (lane >= 32 * g) & (lane < 32 * g + HALO) & (me > 0)
        is_right = (lane >= 32 * g + HALO) & (lane < 32 * g + 2 * HALO) & (me < OWNERS - 1)
        packed = jnp.where(is_left, left, jnp.where(is_right, right, packed))
    edge_ref[own] = packed.astype(jnp.bfloat16)

    def edge_copy(k):
        return remote(
            edge_ref.at[own], edge_ref.at[own], edge_send.at[k], edge_recv.at[k], other(k)[0], me
        )

    def edge_wait(k):
        at = earlier(k)
        remote(
            edge_ref.at[at], edge_ref.at[at], edge_send.at[k], edge_recv.at[k], other(k)[0], me
        ).wait_recv()

    @pl.loop(1, VISITORS)
    def _(k):
        edge_copy(k).start()

    @pl.loop(1, VISITORS)
    def _(k):
        strip_wait(k)
        edge_wait(k)

    @pl.loop(0, VISITORS)
    def _(owner):
        block = edge_ref[owner].astype(jnp.float32)
        for g in range(4):
            at = pl.multiple_of(HALO + owner * 256 + 64 * g, 16)
            moved = pltpu.roll(block, (TILE - 32 * g) % TILE, 1) if g else block
            moved = jnp.where(lane < 2 * HALO, moved, 0.0)
            padded_ref[pl.ds(at, 64), TILE : 2 * TILE] = moved.astype(jnp.bfloat16)

    def store(v, tile, value):
        matched_ref[v * PT + tile] = value

    @pl.loop(0, PT // BLOCK)
    def _(block):
        match_tiles(block, padded_ref, down_ref, w_ref, h_ref, store)

    @pl.loop(1, OWNERS)
    def _(k):
        tile_copy(k).wait_send()

    def back_copy(k):
        to = peer(k)
        return remote(
            outgoing_ref.at[to], returned_ref.at[me], back_send.at[k], back_recv.at[me], visit, to
        )

    def back_wait(k):
        to = origin(k)
        remote(
            outgoing_ref.at[to], returned_ref.at[to], back_send.at[k], back_recv.at[to], visit, to
        ).wait_recv()

    @pl.loop(1, OWNERS)
    def _(k):
        to = peer(k)
        for c in range(CAP):
            outgoing_ref[to, c] = matched_ref[labels_ref[to, 0, c]]
        back_copy(k).start()

    for c in range(CAP):
        returned_ref[me, c] = matched_ref[labels_ref[me, 0, c]]

    @pl.loop(1, OWNERS)
    def _(k):
        back_wait(k)

    @pl.loop(0, VIS * PT)
    def _(n):
        at = position_ref[n]
        value = science_ref[n].astype(jnp.float32) - returned_ref[at // CAP, at % CAP].astype(
            jnp.float32
        )
        out_ref[n] = (value * flag_ref[n]).astype(jnp.bfloat16)

    pair.wait_send()
    for k in (1, 2, 3):
        ring_copy(k).wait_send()
    for n in range(2):
        side_copy(n).wait_send()

    @pl.loop(1, VISITORS)
    def _(k):
        strip_copy(k).wait_send()
        edge_copy(k).wait_send()

    @pl.loop(1, OWNERS)
    def _(k):
        label_copy(k).wait_send()
        weight_copy(k).wait_send()
        back_copy(k).wait_send()


def body(science, tile_ids, valid, weights, kernel_weight_terms, prior_template, prior_weight):
    slots = tile_ids.size
    length = OWNERS * CAP
    ids = tile_ids.reshape(slots)
    flag = valid.reshape(slots).astype(jnp.float32)
    destination = ids // PT
    order = jnp.arange(slots, dtype=jnp.int32)
    label = (order // tile_ids.shape[1]) * PT + ids % PT
    same = (destination[:, None] == destination[None, :]) & (order[:, None] > order[None, :])
    position = destination * CAP + jnp.sum(same.astype(jnp.int32), axis=1)
    placed = position[None, :] == jnp.arange(length, dtype=jnp.int32)[:, None]
    source = jnp.sum(jnp.where(placed, order[None, :], 0), axis=1)
    weighted = weights.reshape(slots).astype(jnp.float32) * flag
    spread = ((0, 0), (0, 0), (0, TILE - CAP))
    labels = jnp.sum(jnp.where(placed, label[None, :], 0), axis=1).reshape(OWNERS, 1, CAP)
    weight = jnp.sum(jnp.where(placed, weighted[None, :], 0.0), axis=1).reshape(OWNERS, 1, CAP)
    across, down = band_constants()
    vmem = pl.BlockSpec(memory_space=pltpu.VMEM)
    smem = pl.BlockSpec(memory_space=pltpu.SMEM)
    hbm = pl.BlockSpec(memory_space=pl.ANY)
    dma = pltpu.SemaphoreType.DMA
    result = pl.pallas_call(
        kernel,
        out_shape=jax.ShapeDtypeStruct((slots, TILE, TILE), jnp.bfloat16),
        in_specs=[smem, smem, smem, smem, vmem, vmem, vmem, hbm, hbm, vmem, vmem],
        out_specs=vmem,
        scratch_shapes=[
            pltpu.VMEM((NPROF, SPAN, GROUP), jnp.bfloat16),
            pltpu.VMEM((NPROF, BLOCK * TILE + 2 * HALO, GROUP), jnp.bfloat16),
            pltpu.VMEM((SKY + 2 * HALO, 2 * TILE), jnp.bfloat16),
            pltpu.VMEM((VIS * PT, TILE, TILE), jnp.bfloat16),
            pltpu.VMEM((OWNERS, CAP, TILE, TILE), jnp.bfloat16),
            pltpu.VMEM((OWNERS, CAP, TILE, TILE), jnp.bfloat16),
            pltpu.VMEM((OWNERS, CAP, TILE, TILE), jnp.bfloat16),
            pltpu.VMEM((PT, ROWS, TILE), jnp.float32),
            pltpu.VMEM((PT // 2, ROWS, TILE), jnp.float32),
            pltpu.VMEM((3, 2, ROWS, TILE), jnp.float32),
            pltpu.VMEM((2, 2 * TILE, TILE), jnp.bfloat16),
            pltpu.VMEM((VISITORS, 64, TILE), jnp.bfloat16),
            pltpu.VMEM((2, 2 * TILE, TILE), jnp.float32),
            pltpu.VMEM((OWNERS, 1, TILE), jnp.int32),
            pltpu.VMEM((OWNERS, 1, TILE), jnp.float32),
            pltpu.SMEM((OWNERS, 1, TILE), jnp.int32),
            pltpu.SMEM((OWNERS, 1, TILE), jnp.float32),
            pltpu.SMEM((PT * CAP,), jnp.float32),
            dma((4,)),
            dma((OWNERS,)),
            dma((OWNERS,)),
            dma((OWNERS,)),
            dma((OWNERS,)),
            dma((OWNERS,)),
            dma((OWNERS,)),
            dma((2,)),
            dma((4,)),
            dma((4,)),
            dma((2,)),
            dma((2,)),
            dma((VISITORS,)),
            dma((VISITORS,)),
            dma((VISITORS,)),
            dma((VISITORS,)),
            dma((OWNERS,)),
            dma((OWNERS,)),
        ],
        compiler_params=pltpu.CompilerParams(
            vmem_limit_bytes=56 << 20, collective_id=0, has_side_effects=True
        ),
    )(
        source,
        position,
        flag,
        kernel_weight_terms.astype(jnp.float32),
        science.reshape(slots, TILE, TILE),
        jnp.pad(labels, spread),
        jnp.pad(weight, spread),
        prior_template,
        prior_weight,
        jnp.asarray(across),
        jnp.asarray(down),
    )
    return result.reshape(science.shape)


def solution(mesh):
    placed = (
        P("visit", "patch", None, None),
        P("visit", "patch"),
        P("visit", "patch"),
        P("visit", "patch"),
        P("visit", None, None),
        P(None, "patch"),
        P(None, "patch"),
    )
    return jax.shard_map(
        body, mesh=mesh, in_specs=placed, out_specs=P("visit", "patch", None, None), check_vma=False
    )
```

time: 221 us -> 137 us (0.62)
  the two profiles are of different devices: /device:TPU:0 before, /device:TPU:56 now
where the time goes in v1:
time: 137 us
  Pallas kernels  129 us (94%)
  local copies, waits for them, and re-layouts  6.43 us (5%)
  other arithmetic  1.52 us (1%)
    pallas_call x1, Pallas kernels, body(): pl.pallas_call(kernel, out_shape=jax.ShapeDtypeStruct((slots, TILE, TILE)...  129 us
    unnamed x13, local copies, waits for them, and re-layouts  4.81 us

profile of v1, /device:TPU:56, one launch (start us, length us, event | category | flops | bytes accessed | tf_op | source)
XLA Modules:
  0.0 136.9 jit_solution(14919763577472743292)
XLA Ops:
  0.0 0.0 copy-start.4
  0.0 0.7 copy-done.4
  0.7 0.0 copy-start.5
  0.7 0.1 reshape.136
  0.8 0.6 copy-done.5
  1.3 0.1 reshape.141
  1.4 0.2 convert_reduce_fusion
  1.6 0.0 copy-start.1
  1.6 0.6 select_reduce_fusion.1
  2.3 0.0 copy-start.2
  2.3 0.7 copy-done.2
  2.9 0.1 convert_element_type.25.flag_ref
  3.0 0.0 copy-done.1
  3.0 0.5 copy-done.3
  3.5 0.1 select_reduce_fusion
  3.6 0.1 reshape.139
  3.7 0.6 pad.9.weight_ref
  4.3 0.1 reshape.138
  4.4 0.0 copy-start
  4.4 0.6 pad.8.label_ref
  5.0 0.1 copy-done
  5.1 0.6 copy_convert_fusion.kw_ref
  5.7 128.9 %shard_map.91 = bf16[32,128,128]{2,1,0:T(8,128)(2,1)} custom-call(s32[64]{0:T(128)} %get-tuple-element.6.source_ref, s32[32]{0:T(128)} %copy-done.1, f32[32]{0:T(128)} %copy-done.3, f32[2,6,25]{2,1,0:T(8,128)} %copy_convert_fusion.kw_ref, bf16[32,128,128]{2,1,0:T(8,128)(2,1)} %bitcast.5, s32[16,1,128]{2,1,0:T(1,128)} %pad.8.label_ref, ...), custom_call_target="tpu_custom_call" | custom-call | tf_op jit(solution)/shard_map/pallas_call | solution.py:474
  134.6 2.3 %copy.21 = bf16[2,16,128,128]{3,2,1,0:T(8,128)(2,1)} copy(bf16[2,16,128,128]{3,2,1,0:T(8,128)(2,1)} %bitcast.4) | data formatting | bytes 2097152
  (5 shorter events, 0.0 us)
Async XLA Ops:
  0.0 0.7 copy-start.4
  0.7 0.7 copy-start.5
  1.6 1.4 %copy-start.1 = (s32[32]{0:T(128)}, s32[32]{0:T(128)S(1)}, u32[]{:S(2)}) copy-start(s32[32]{0:T(128)S(1)} %multiply_add_fusion.position_ref) | copy-start | bytes 388
  2.3 0.7 copy-start.2
  3.0 0.5 copy-start.3
  4.4 0.7 copy-start

commit v2 on v0

v2 whole, which is shorter than its diff:
```python
import jax
import jax.numpy as jnp
import ml_dtypes
import numpy as np
from jax import lax
from jax.experimental import pallas as pl
from jax.experimental.pallas import tpu as pltpu
from jax.sharding import PartitionSpec as P

TILE = 128
KHALF = 15
HALO = 16
SPAN = TILE + 2 * HALO
SIGMAS = (1.5, 3.0, 5.0, 7.0)
DEGREES = (4, 2, 1, 0)
NPROF = 11
NBASIS = 25
NPOLY = 6
PT = 16
SKY = 2048
VIS = 2
GROUP = 3 * VIS * TILE
CH = 32
CHUNKS = TILE // CH
MAIN = NPROF * TILE
DEEP = MAIN + 3 * TILE
OWNERS = 16
VISITORS = 8
CAP = 4
MESH = pl.DeviceIdType.MESH


def profile_table():
    u = np.arange(-KHALF, KHALF + 1, dtype=np.float32)
    rows = []
    for sigma, degree in zip(SIGMAS, DEGREES):
        scaled = u / np.float32(sigma)
        envelope = np.exp(np.float32(-0.5) * scaled * scaled)
        for power in range(degree + 1):
            shaped = envelope * scaled**power
            rows.append(shaped / np.sum(np.abs(shaped)))
    return np.stack(rows).astype(np.float32)


def band_constants():
    profiles = profile_table()
    target = np.arange(TILE)

    def band(source):
        taps = source[:, None] - target[None, :] + KHALF
        inside = (taps >= 0) & (taps <= 2 * KHALF)
        return np.where(inside[None], profiles[:, np.clip(taps, 0, 2 * KHALF)], 0.0)

    columns = np.concatenate(
        [np.arange(TILE), np.arange(-HALO, 0), np.arange(TILE, TILE + HALO)]
    )
    across = band(columns).astype(ml_dtypes.bfloat16)
    down = band(np.arange(-HALO, CH + HALO))[:, :, :CH].transpose(0, 2, 1)
    down = down.reshape(NPROF * CH, CH + 2 * HALO).astype(ml_dtypes.bfloat16)
    return across, down


def basis_order():
    order, start = [], 0
    for degree in DEGREES:
        for j in range(degree + 1):
            order.append((start + j, [start + i for i in range(degree - j + 1)]))
        start += degree + 1
    return order


def build_weights(strip, kw_ref, across_ref, w_ref):
    lane = lax.broadcasted_iota(jnp.int32, (1, TILE), 1) + strip * TILE
    x = (lane.astype(jnp.float32) + 0.5) / SKY * 2.0 - 1.0
    xx = x * x
    unused = MAIN + NPROF * 2 * HALO
    w_ref[unused:, :] = jnp.zeros((DEEP - unused, GROUP), jnp.bfloat16)
    k = 0
    for j, sources in basis_order():
        for v in range(VIS):
            sums = [None, None, None]
            for n, source in enumerate(sources):
                c = [kw_ref[v, m, k + n] for m in range(NPOLY)]
                rows = (c[0] + c[1] * x + c[3] * xx, c[2] + c[4] * x, c[5])
                image = across_ref[source].astype(jnp.float32)
                for b in range(3):
                    term = rows[b] * image
                    sums[b] = term if sums[b] is None else sums[b] + term
            for b in range(3):
                at = (b * VIS + v) * TILE
                value = sums[b].astype(jnp.bfloat16)
                halo = MAIN + j * 2 * HALO
                w_ref[j * TILE : (j + 1) * TILE, at : at + TILE] = value[:TILE]
                w_ref[halo : halo + 2 * HALO, at : at + TILE] = value[TILE:]
        k += len(sources)


def match_chunk(part, padded_ref, down_ref, w_ref, columns_ref, matched_ref):
    @pl.loop(0, PT, unroll=True)
    def _(tile):
        top = pl.multiple_of(tile * TILE + part * CH, 16)
        rows = pl.ds(pl.multiple_of(tile * CH, 16), CH)
        both = jnp.dot(
            down_ref[...],
            padded_ref[pl.ds(top, CH + 2 * HALO), :],
            preferred_element_type=jnp.float32,
        )
        for group in range(3):
            total = None
            for q in range(min(4, NPROF - 4 * group)):
                j = 4 * group + q
                piece = both[j * CH : (j + 1) * CH]
                columns_ref[rows, j * TILE : (j + 1) * TILE] = piece[:, :TILE].astype(jnp.bfloat16)
                side = piece[:, TILE:]
                side = pltpu.roll(side, 2 * HALO * q, 1) if q else side
                total = side if total is None else total + side
            at = MAIN + group * TILE
            columns_ref[rows, at : at + TILE] = total.astype(jnp.bfloat16)

    half = VIS * TILE
    line = lax.broadcasted_iota(jnp.int32, (PT * CH, 1), 0)
    y = (line // CH * TILE + part * CH + line % CH).astype(jnp.float32)
    y = (y + 0.5) / SKY * 2.0 - 1.0
    total = jnp.zeros((PT * CH, half), jnp.float32)
    for power, factor in enumerate((None, y, y * y)):
        term = jnp.dot(
            columns_ref[...],
            w_ref[:, power * half : (power + 1) * half],
            preferred_element_type=jnp.float32,
        )
        total = total + (term if factor is None else factor * term)
    total = total.astype(jnp.bfloat16)
    for v in range(VIS):
        for tile in range(PT):
            matched_ref[v * PT + tile] = total[
                tile * CH : (tile + 1) * CH, v * TILE : (v + 1) * TILE
            ]


def remote(src, dst, send, recv, visit, patch):
    return pltpu.make_async_remote_copy(
        src_ref=src,
        dst_ref=dst,
        send_sem=send,
        recv_sem=recv,
        device_id={"visit": visit, "patch": patch},
        device_id_type=MESH,
    )


def kernel(
    source_ref, position_ref, flag_ref, kw_ref, science_ref, label_ref, weight_ref,
    prior_ref, prior_weight_ref, across_ref, down_ref, out_ref,
    w_ref, columns_ref, padded_ref, matched_ref, outgoing_ref, arrived_ref,
    back_0, back_1, back_2, back_3,
    acc_ref, pair_ref, ring_ref, side_ref, sum_ref, sum_pair_ref, sum_ring_ref,
    prior_vmem, labels_vmem, weights_vmem, labels_ref, weights_ref, coef_ref,
    local_sem, label_send, label_recv, weight_send, weight_recv, tile_send, tile_recv,
    pair_send, pair_recv, ring_send, ring_recv, side_send, side_recv, strip_send, strip_recv,
    sum_send, sum_recv, back_send, back_recv,
):
    visit = lax.axis_index("visit")
    me = lax.axis_index("patch")
    z, core = visit // 2, visit % 2
    twin = z * 2 + 1 - core
    returned = (back_0, back_1, back_2, back_3)
    own = core * 4 + z

    def peer(k):
        return lax.rem(me + k, OWNERS)

    def origin(k):
        return lax.rem(me + OWNERS - k, OWNERS)

    def other(k):
        return lax.rem(visit + k, VISITORS)

    def earlier(k):
        to = lax.rem(visit + VISITORS - k, VISITORS)
        return (to % 2) * 4 + to // 2

    prior_copies = [
        pltpu.make_async_copy(
            ref.at[pl.ds(pl.multiple_of(own * 256, 256), 256), :],
            prior_vmem.at[n],
            local_sem.at[n],
        )
        for n, ref in enumerate((prior_ref, prior_weight_ref))
    ]
    for copy in prior_copies:
        copy.start()

    barrier = pltpu.get_barrier_semaphore()

    @pl.loop(1, OWNERS)
    def _(k):
        pl.semaphore_signal(
            barrier, inc=1, device_id={"visit": visit, "patch": peer(k)}, device_id_type=MESH
        )

    @pl.loop(1, VISITORS)
    def _(k):
        pl.semaphore_signal(
            barrier, inc=1, device_id={"visit": other(k), "patch": me}, device_id_type=MESH
        )

    pl.semaphore_wait(barrier, OWNERS + VISITORS - 2)

    def label_copies(k, to, slot):
        return (
            remote(
                label_ref.at[to], labels_vmem.at[slot], label_send.at[k], label_recv.at[slot],
                visit, to,
            ),
            remote(
                weight_ref.at[to], weights_vmem.at[slot], weight_send.at[k], weight_recv.at[slot],
                visit, to,
            ),
        )

    def tile_copy(part, k, to, slot):
        return remote(
            outgoing_ref.at[part, to], arrived_ref.at[part, slot],
            tile_send.at[part, k], tile_recv.at[part, slot], visit, to,
        )

    def back_copy(part, k, to, slot):
        return remote(
            outgoing_ref.at[part, to], returned[part].at[slot],
            back_send.at[part, k], back_recv.at[part, slot], visit, to,
        )

    @pl.loop(1, OWNERS)
    def _(k):
        for copy in label_copies(k, peer(k), me):
            copy.start()

    def pack(part, to, target, at):
        rows = pl.ds(pl.multiple_of(part * CH, 16), CH)
        for c in range(CAP):
            target[part, at, c] = science_ref[source_ref[to * CAP + c], rows, :]

    @pl.loop(0, CHUNKS)
    def _(part):
        @pl.loop(1, OWNERS)
        def _(k):
            pack(part, peer(k), outgoing_ref, peer(k))
            tile_copy(part, k, peer(k), me).start()

        pack(part, me, arrived_ref, me)

    labels_vmem[me] = label_ref[me]
    weights_vmem[me] = weight_ref[me]

    @pl.loop(1, OWNERS)
    def _(k):
        for copy in label_copies(k, origin(k), origin(k)):
            copy.wait_recv()

    scalars = [
        pltpu.make_async_copy(labels_vmem, labels_ref, local_sem.at[2]),
        pltpu.make_async_copy(weights_vmem, weights_ref, local_sem.at[3]),
    ]
    for copy in scalars:
        copy.start()
    acc_ref[...] = jnp.zeros_like(acc_ref)
    sum_ref[...] = jnp.zeros_like(sum_ref)
    blank = jnp.zeros((HALO, 2 * TILE), jnp.bfloat16)
    padded_ref[:HALO, :] = blank
    padded_ref[HALO + SKY :, :] = blank
    for copy in scalars:
        copy.wait()

    @pl.loop(0, OWNERS)
    def _(at):
        for t in range(PT):
            total = 0.0
            for c in range(CAP):
                value = jnp.where(labels_ref[at, 0, c] % PT == t, weights_ref[at, 0, c], 0.0)
                coef_ref[(at * PT + t) * CAP + c] = value
                total = total + value
            sum_ref[t] += jnp.full((8, TILE), total, jnp.float32)

    sum_copy = remote(
        sum_ref.at[pl.ds((1 - core) * 8, 8)], sum_pair_ref, sum_send.at[0], sum_recv.at[0], twin, me
    )

    def sum_ring(k):
        to = lax.rem(z + k, 4)
        return remote(
            sum_ref.at[pl.ds(core * 8 + to * 2, 2)], sum_ring_ref.at[k - 1],
            sum_send.at[k], sum_recv.at[k], to * 2 + core, me,
        )

    sum_copy.start()
    build_weights(me, kw_ref, across_ref, w_ref)
    sum_copy.wait_recv()
    for n in range(8):
        sum_ref[core * 8 + n] += sum_pair_ref[n]
    for k in (1, 2, 3):
        sum_ring(k).start()
    for copy in prior_copies:
        copy.wait()

    def pair_copy(part):
        return remote(
            acc_ref.at[part, pl.ds((1 - core) * 8, 8)], pair_ref.at[part],
            pair_send.at[part], pair_recv.at[part], twin, me,
        )

    def ring_copy(part, k):
        to = lax.rem(z + k, 4)
        return remote(
            acc_ref.at[part, pl.ds(core * 8 + to * 2, 2)], ring_ref.at[part, k - 1],
            ring_send.at[part, k], ring_recv.at[part, k], to * 2 + core, me,
        )

    def lines(part, owner, n):
        return pl.multiple_of(HALO + owner * 256 + n * TILE + part * CH, 16)

    def side_copy(part, n, side):
        to = peer(1) if side == 0 else origin(1)
        return remote(
            padded_ref.at[pl.ds(lines(part, own, n), CH), pl.ds(0, TILE)],
            side_ref.at[part, side, n],
            side_send.at[part, side, n], side_recv.at[part, side, n], visit, to,
        )

    def strip_copy(part, n, k, owner):
        rows = padded_ref.at[pl.ds(lines(part, owner, n), CH), :]
        return remote(
            rows, rows, strip_send.at[part, n, k], strip_recv.at[part, n, k], other(k), me
        )

    def gather(part):
        @pl.loop(0, OWNERS)
        def _(k):
            at = origin(k)

            @pl.when(k > 0)
            def _():
                tile_copy(part, k, at, at).wait_recv()

            slots = [arrived_ref[part, at, c].astype(jnp.float32) for c in range(CAP)]
            for t in range(PT):
                value = acc_ref[part, t]
                for c in range(CAP):
                    value = value + coef_ref[(at * PT + t) * CAP + c] * slots[c]
                acc_ref[part, t] = value

        pair_copy(part).start()

    def reduce_pair(part):
        pair_copy(part).wait_recv()
        for k in (1, 2, 3, 0):
            to = lax.rem(z + k, 4)
            for n in range(2):
                acc_ref[part, core * 8 + to * 2 + n] += pair_ref[part, to * 2 + n]
            if k > 0:
                ring_copy(part, k).start()

    def finish_template(part):
        for k in (1, 2, 3):
            ring_copy(part, k).wait_recv()
        for n in range(2):
            total = acc_ref[part, own * 2 + n]
            weight_sum = sum_ref[own * 2 + n]
            for k in range(3):
                total = total + ring_ref[part, k, n]
                weight_sum = weight_sum + sum_ring_ref[k, n]
            rows = pl.ds(pl.multiple_of(n * TILE + part * CH, 16), CH)
            weight = prior_vmem[1, rows, :]
            template = (weight * prior_vmem[0, rows, :] + total) / (weight + weight_sum[:1])
            padded_ref[pl.ds(lines(part, own, n), CH), :TILE] = template.astype(jnp.bfloat16)
        for n in range(2):
            for side in range(2):
                side_copy(part, n, side).start()

    def spread_strip(part):
        lane = lax.broadcasted_iota(jnp.int32, (CH, TILE), 1)
        for n in range(2):
            for side in range(2):
                side_copy(part, n, side).wait_recv()
            left = pltpu.roll(side_ref[part, 0, n].astype(jnp.float32), HALO, 1)
            right = pltpu.roll(side_ref[part, 1, n].astype(jnp.float32), HALO, 1)
            halo = jnp.where(
                (lane < HALO) & (me > 0),
                left,
                jnp.where(
                    (lane >= HALO) & (lane < 2 * HALO) & (me < OWNERS - 1), right, 0.0
                ),
            )
            padded_ref[pl.ds(lines(part, own, n), CH), TILE:] = halo.astype(jnp.bfloat16)

            @pl.loop(1, VISITORS)
            def _(k):
                strip_copy(part, n, k, own).start()

    def wait_strips(part):
        @pl.loop(1, VISITORS)
        def _(k):
            for n in range(2):
                strip_copy(part, n, k, earlier(k)).wait_recv()

    @pl.loop(0, CHUNKS + 3)
    def _(step):
        @pl.when(step < CHUNKS)
        def _():
            gather(step)

        @pl.when((step >= 1) & (step < CHUNKS + 1))
        def _():
            reduce_pair(step - 1)

        @pl.when(step == 2)
        def _():
            for k in (1, 2, 3):
                sum_ring(k).wait_recv()

        @pl.when((step >= 2) & (step < CHUNKS + 2))
        def _():
            finish_template(step - 2)

        @pl.when(step >= 3)
        def _():
            spread_strip(step - 3)

    @pl.loop(0, CHUNKS)
    def _(part):
        @pl.loop(1, OWNERS)
        def _(k):
            tile_copy(part, k, peer(k), me).wait_send()

    @pl.loop(0, CHUNKS)
    def _(step):
        part = lax.rem(step + 1, CHUNKS)

        @pl.when(step == 0)
        def _():
            for early in range(CHUNKS - 1):
                wait_strips(early)

        @pl.when(step == 1)
        def _():
            wait_strips(CHUNKS - 1)

        match_chunk(part, padded_ref, down_ref, w_ref, columns_ref, matched_ref)

        @pl.loop(1, OWNERS)
        def _(k):
            to = peer(k)
            for c in range(CAP):
                outgoing_ref[part, to, c] = matched_ref[labels_ref[to, 0, c]]
            for q in range(CHUNKS):

                @pl.when(part == q)
                def _():
                    back_copy(q, k, to, me).start()

        for q in range(CHUNKS):

            @pl.when(part == q)
            def _():
                for c in range(CAP):
                    returned[q][me, c] = matched_ref[labels_ref[me, 0, c]]

    for step in range(CHUNKS):
        part = (step + 1) % CHUNKS
        rows = pl.ds(part * CH, CH)

        @pl.loop(1, OWNERS)
        def _(k):
            back_copy(part, k, origin(k), origin(k)).wait_recv()

        @pl.loop(0, VIS * PT)
        def _(n):
            at = position_ref[n]
            matched = returned[part][at // CAP, at % CAP].astype(jnp.float32)
            value = science_ref[n, rows, :].astype(jnp.float32) - matched
            out_ref[n, rows, :] = (value * flag_ref[n]).astype(jnp.bfloat16)

    sum_copy.wait_send()
    for k in (1, 2, 3):
        sum_ring(k).wait_send()

    @pl.loop(0, CHUNKS)
    def _(part):
        pair_copy(part).wait_send()
        for k in (1, 2, 3):
            ring_copy(part, k).wait_send()
        for n in range(2):
            for side in range(2):
                side_copy(part, n, side).wait_send()

            @pl.loop(1, VISITORS)
            def _(k):
                strip_copy(part, n, k, own).wait_send()

    for part in range(CHUNKS):

        @pl.loop(1, OWNERS)
        def _(k):
            back_copy(part, k, peer(k), me).wait_send()

    @pl.loop(1, OWNERS)
    def _(k):
        for copy in label_copies(k, peer(k), me):
            copy.wait_send()


def body(science, tile_ids, valid, weights, kernel_weight_terms, prior_template, prior_weight):
    slots = tile_ids.size
    length = OWNERS * CAP
    ids = tile_ids.reshape(slots)
    flag = valid.reshape(slots).astype(jnp.float32)
    destination = ids // PT
    order = jnp.arange(slots, dtype=jnp.int32)
    label = (order // tile_ids.shape[1]) * PT + ids % PT
    same = (destination[:, None] == destination[None, :]) & (order[:, None] > order[None, :])
    position = destination * CAP + jnp.sum(same.astype(jnp.int32), axis=1)
    placed = position[None, :] == jnp.arange(length, dtype=jnp.int32)[:, None]
    source = jnp.sum(jnp.where(placed, order[None, :], 0), axis=1)
    weighted = weights.reshape(slots).astype(jnp.float32) * flag
    spread = ((0, 0), (0, 0), (0, TILE - CAP))
    labels = jnp.sum(jnp.where(placed, label[None, :], 0), axis=1).reshape(OWNERS, 1, CAP)
    weight = jnp.sum(jnp.where(placed, weighted[None, :], 0.0), axis=1).reshape(OWNERS, 1, CAP)
    across, down = band_constants()
    vmem = pl.BlockSpec(memory_space=pltpu.VMEM)
    smem = pl.BlockSpec(memory_space=pltpu.SMEM)
    hbm = pl.BlockSpec(memory_space=pl.ANY)
    dma = pltpu.SemaphoreType.DMA
    result = pl.pallas_call(
        kernel,
        out_shape=jax.ShapeDtypeStruct((slots, TILE, TILE), jnp.bfloat16),
        in_specs=[smem, smem, smem, smem, vmem, vmem, vmem, hbm, hbm, vmem, vmem],
        out_specs=vmem,
        scratch_shapes=[
            pltpu.VMEM((DEEP, GROUP), jnp.bfloat16),
            pltpu.VMEM((PT * CH, DEEP), jnp.bfloat16),
            pltpu.VMEM((SKY + 2 * HALO, 2 * TILE), jnp.bfloat16),
            pltpu.VMEM((VIS * PT, CH, TILE), jnp.bfloat16),
            pltpu.VMEM((CHUNKS, OWNERS, CAP, CH, TILE), jnp.bfloat16),
            pltpu.VMEM((CHUNKS, OWNERS, CAP, CH, TILE), jnp.bfloat16),
            pltpu.VMEM((OWNERS, CAP, CH, TILE), jnp.bfloat16),
            pltpu.VMEM((OWNERS, CAP, CH, TILE), jnp.bfloat16),
            pltpu.VMEM((OWNERS, CAP, CH, TILE), jnp.bfloat16),
            pltpu.VMEM((OWNERS, CAP, CH, TILE), jnp.bfloat16),
            pltpu.VMEM((CHUNKS, PT, CH, TILE), jnp.float32),
            pltpu.VMEM((CHUNKS, PT // 2, CH, TILE), jnp.float32),
            pltpu.VMEM((CHUNKS, 3, 2, CH, TILE), jnp.float32),
            pltpu.VMEM((CHUNKS, 2, 2, CH, TILE), jnp.bfloat16),
            pltpu.VMEM((PT, 8, TILE), jnp.float32),
            pltpu.VMEM((PT // 2, 8, TILE), jnp.float32),
            pltpu.VMEM((3, 2, 8, TILE), jnp.float32),
            pltpu.VMEM((2, 2 * TILE, TILE), jnp.float32),
            pltpu.VMEM((OWNERS, 1, TILE), jnp.int32),
            pltpu.VMEM((OWNERS, 1, TILE), jnp.float32),
            pltpu.SMEM((OWNERS, 1, TILE), jnp.int32),
            pltpu.SMEM((OWNERS, 1, TILE), jnp.float32),
            pltpu.SMEM((OWNERS * PT * CAP,), jnp.float32),
            dma((4,)),
            dma((OWNERS,)),
            dma((OWNERS,)),
            dma((OWNERS,)),
            dma((OWNERS,)),
            dma((CHUNKS, OWNERS)),
            dma((CHUNKS, OWNERS)),
            dma((CHUNKS,)),
            dma((CHUNKS,)),
            dma((CHUNKS, 4)),
            dma((CHUNKS, 4)),
            dma((CHUNKS, 2, 2)),
            dma((CHUNKS, 2, 2)),
            dma((CHUNKS, 2, VISITORS)),
            dma((CHUNKS, 2, VISITORS)),
            dma((4,)),
            dma((4,)),
            dma((CHUNKS, OWNERS)),
            dma((CHUNKS, OWNERS)),
        ],
        compiler_params=pltpu.CompilerParams(
            vmem_limit_bytes=56 << 20, collective_id=0, has_side_effects=True
        ),
    )(
        source,
        position,
        flag,
        kernel_weight_terms.astype(jnp.float32),
        science.reshape(slots, TILE, TILE),
        jnp.pad(labels, spread),
        jnp.pad(weight, spread),
        prior_template,
        prior_weight,
        jnp.asarray(across),
        jnp.asarray(down),
    )
    return result.reshape(science.shape)


def solution(mesh):
    placed = (
        P("visit", "patch", None, None),
        P("visit", "patch"),
        P("visit", "patch"),
        P("visit", "patch"),
        P("visit", None, None),
        P(None, "patch"),
        P(None, "patch"),
    )
    return jax.shard_map(
        body, mesh=mesh, in_specs=placed, out_specs=P("visit", "patch", None, None), check_vma=False
    )
```

time: 221 us -> 95.6 us (0.43); the launches traced: 218 us -> 95.4 us
  waiting for transfers between devices: 120 us -> 0 us
  Pallas kernels: 26.6 us -> 87.4 us
  starting transfers between devices: 24.1 us -> 0 us
  between operations: 13.7 us -> 0.04 us
  blocking collectives: 13.3 us -> 0 us
  other arithmetic: 9.92 us -> 1.52 us
  local copies, waits for them, and re-layouts: 9.13 us -> 6.43 us
    pallas_call x1, Pallas kernels: 26.6 us -> 87.4 us  [body(): pl.pallas_call(kernel, out_shape=jax.ShapeDtypeStruct((slots, TILE, TILE)...]
    all_to_all x3 -> x0, waiting for transfers between devices: 59.5 us -> none  [the longest x1 29 us: body(): lax.all_to_all(outgoing, 'patch', split_axis=0, concat_axis=0, tiled=True)]
    psum x1 -> x0, waiting for transfers between devices: 48.6 us -> none  [body(): total, total_weight = lax.psum((numerator, weight_rows), 'visit')]
    all_to_all x3 -> x0, starting transfers between devices: 19.2 us -> none  [the longest x1 8.37 us: body(): lax.all_to_all(chosen, 'patch', split_axis=0, concat_axis=0, tiled=True)]
    psum x1 -> x0, blocking collectives: 13.3 us -> none  [body(): total, total_weight = lax.psum((numerator, weight_rows), 'visit')]
    ppermute x2 -> x0, waiting for transfers between devices: 11.9 us -> none  [the longest x1 7.8 us: body(): left = lax.ppermute(template[:, TILE - HALO:], 'patch', up)]
    gather x5 -> x0, local copies, waits for them, and re-layouts: 5.63 us -> none  [the longest x1 2.18 us: body(): jnp.take(pixels, source_slot, axis=0)]
    ppermute x2 -> x0, starting transfers between devices: 4.85 us -> none  [the longest x1 3.55 us: body(): left = lax.ppermute(template[:, TILE - HALO:], 'patch', up)]
  transfers between devices with their start and end apart: 6 -> 0, of which waited for: 6 -> 0; matrix products, arithmetic and copies ran while one was open for 2% -> 0% of each run, Pallas kernels for 0% -> 0%
where the time goes in v2:
time: 95.6 us; the launch traced here: 95.4 us
  Pallas kernels  87.4 us (91%)
  local copies, waits for them, and re-layouts  6.43 us (7%)
  other arithmetic  1.52 us (2%)
    pallas_call x1, Pallas kernels, body(): pl.pallas_call(kernel, out_shape=jax.ShapeDtypeStruct((slots, TILE, TILE)...  87.4 us
    unnamed x13, local copies, waits for them, and re-layouts  4.81 us

profile of v2, /device:TPU:0, one launch (start us, length us, event | category | flops | bytes accessed | tf_op | source)
XLA Modules:
  0.0 95.4 jit_solution(2776506272455835803)
XLA Ops:
  0.0 0.0 copy-start.4
  0.0 0.7 copy-done.4
  0.7 0.0 copy-start.5
  0.7 0.1 reshape.136
  0.8 0.6 copy-done.5
  1.3 0.1 reshape.141
  1.4 0.2 convert_reduce_fusion
  1.6 0.0 copy-start.1
  1.6 0.6 select_reduce_fusion.1
  2.3 0.0 copy-start.2
  2.3 0.7 copy-done.2
  2.9 0.1 convert_element_type.25.flag_ref
  3.0 0.0 copy-start.3
  3.0 0.0 copy-done.1
  3.0 0.5 copy-done.3
  3.5 0.1 select_reduce_fusion
  3.6 0.1 reshape.139
  3.7 0.6 pad.9.weight_ref
  4.3 0.1 reshape.138
  4.4 0.6 pad.8.label_ref
  5.0 0.1 copy-done
  5.1 0.6 copy_convert_fusion.kw_ref
  5.7 87.4 %shard_map.91 = bf16[32,128,128]{2,1,0:T(8,128)(2,1)} custom-call(s32[64]{0:T(128)} %get-tuple-element.6.source_ref, s32[32]{0:T(128)} %copy-done.1, f32[32]{0:T(128)} %copy-done.3, f32[2,6,25]{2,1,0:T(8,128)} %copy_convert_fusion.kw_ref, bf16[32,128,128]{2,1,0:T(8,128)(2,1)} %bitcast.5, s32[16,1,128]{2,1,0:T(1,128)} %pad.8.label_ref, ...), custom_call_target="tpu_custom_call" | custom-call | tf_op jit(solution)/shard_map/pallas_call | solution.py:532
  93.1 2.3 %copy.21 = bf16[2,16,128,128]{3,2,1,0:T(8,128)(2,1)} copy(bf16[2,16,128,128]{3,2,1,0:T(8,128)(2,1)} %bitcast.4) | data formatting | bytes 2097152
  (5 shorter events, 0.0 us)
Async XLA Ops:
  0.0 0.7 copy-start.4
  0.7 0.7 copy-start.5
  1.6 1.4 %copy-start.1 = (s32[32]{0:T(128)}, s32[32]{0:T(128)S(1)}, u32[]{:S(2)}) copy-start(s32[32]{0:T(128)S(1)} %multiply_add_fusion.position_ref) | copy-start | bytes 388
  2.3 0.7 copy-start.2
  3.0 0.5 copy-start.3
  4.4 0.7 copy-start

commit v3 on v2

v3 whole, which is shorter than its diff:
```python
import jax
import jax.numpy as jnp
import ml_dtypes
import numpy as np
from jax import lax
from jax.experimental import pallas as pl
from jax.experimental.pallas import tpu as pltpu
from jax.sharding import PartitionSpec as P

TILE = 128
KHALF = 15
HALO = 16
SPAN = TILE + 2 * HALO
SIGMAS = (1.5, 3.0, 5.0, 7.0)
DEGREES = (4, 2, 1, 0)
NPROF = 11
NBASIS = 25
NPOLY = 6
PT = 16
SKY = 2048
VIS = 2
GROUP = 3 * VIS * TILE
CH = 32
CHUNKS = TILE // CH
MAIN = NPROF * TILE
DEEP = MAIN + 3 * TILE
OWNERS = 16
VISITORS = 8
CAP = 4
MESH = pl.DeviceIdType.MESH


def profile_table():
    u = np.arange(-KHALF, KHALF + 1, dtype=np.float32)
    rows = []
    for sigma, degree in zip(SIGMAS, DEGREES):
        scaled = u / np.float32(sigma)
        envelope = np.exp(np.float32(-0.5) * scaled * scaled)
        for power in range(degree + 1):
            shaped = envelope * scaled**power
            rows.append(shaped / np.sum(np.abs(shaped)))
    return np.stack(rows).astype(np.float32)


def band_constants():
    profiles = profile_table()
    target = np.arange(TILE)

    def band(source):
        taps = source[:, None] - target[None, :] + KHALF
        inside = (taps >= 0) & (taps <= 2 * KHALF)
        return np.where(inside[None], profiles[:, np.clip(taps, 0, 2 * KHALF)], 0.0)

    columns = np.concatenate(
        [np.arange(TILE), np.arange(-HALO, 0), np.arange(TILE, TILE + HALO)]
    )
    across = band(columns).astype(ml_dtypes.bfloat16)
    down = band(np.arange(-HALO, CH + HALO))[:, :, :CH].transpose(0, 2, 1)
    down = down.reshape(NPROF * CH, CH + 2 * HALO).astype(ml_dtypes.bfloat16)
    return across, down


def basis_order():
    order, start = [], 0
    for degree in DEGREES:
        for j in range(degree + 1):
            order.append((start + j, [start + i for i in range(degree - j + 1)]))
        start += degree + 1
    return order


def build_weights(strip, kw_ref, across_ref, w_ref):
    lane = lax.broadcasted_iota(jnp.int32, (1, TILE), 1) + strip * TILE
    x = (lane.astype(jnp.float32) + 0.5) / SKY * 2.0 - 1.0
    xx = x * x
    unused = MAIN + NPROF * 2 * HALO
    w_ref[unused:, :] = jnp.zeros((DEEP - unused, GROUP), jnp.bfloat16)
    k = 0
    for j, sources in basis_order():
        for v in range(VIS):
            sums = [None, None, None]
            for n, source in enumerate(sources):
                c = [kw_ref[v, m, k + n] for m in range(NPOLY)]
                rows = (c[0] + c[1] * x + c[3] * xx, c[2] + c[4] * x, c[5])
                image = across_ref[source].astype(jnp.float32)
                for b in range(3):
                    term = rows[b] * image
                    sums[b] = term if sums[b] is None else sums[b] + term
            for b in range(3):
                at = (b * VIS + v) * TILE
                value = sums[b].astype(jnp.bfloat16)
                halo = MAIN + j * 2 * HALO
                w_ref[j * TILE : (j + 1) * TILE, at : at + TILE] = value[:TILE]
                w_ref[halo : halo + 2 * HALO, at : at + TILE] = value[TILE:]
        k += len(sources)


def match_chunk(part, padded_ref, down_ref, w_ref, columns_ref, matched_ref):
    first = (part == 0).astype(jnp.int32)
    last = (part == CHUNKS - 1).astype(jnp.int32)
    before = lax.rem(part + CHUNKS - 1, CHUNKS)
    after = lax.rem(part + 1, CHUNKS)

    @pl.loop(0, PT, unroll=True)
    def _(tile):
        rows = pl.ds(pl.multiple_of(tile * CH, 16), CH)
        window = jnp.concatenate(
            [
                padded_ref[before, tile + 1 - first, CH - HALO :, :],
                padded_ref[part, tile + 1],
                padded_ref[after, tile + 1 + last, :HALO, :],
            ],
            axis=0,
        )
        both = jnp.dot(down_ref[...], window, preferred_element_type=jnp.float32)
        for group in range(3):
            total = None
            for q in range(min(4, NPROF - 4 * group)):
                j = 4 * group + q
                piece = both[j * CH : (j + 1) * CH]
                columns_ref[rows, j * TILE : (j + 1) * TILE] = piece[:, :TILE].astype(jnp.bfloat16)
                side = piece[:, TILE:]
                side = pltpu.roll(side, 2 * HALO * q, 1) if q else side
                total = side if total is None else total + side
            at = MAIN + group * TILE
            columns_ref[rows, at : at + TILE] = total.astype(jnp.bfloat16)

    half = VIS * TILE
    line = lax.broadcasted_iota(jnp.int32, (PT * CH, 1), 0)
    y = (line // CH * TILE + part * CH + line % CH).astype(jnp.float32)
    y = (y + 0.5) / SKY * 2.0 - 1.0
    total = jnp.zeros((PT * CH, half), jnp.float32)
    for power, factor in enumerate((None, y, y * y)):
        term = jnp.dot(
            columns_ref[...],
            w_ref[:, power * half : (power + 1) * half],
            preferred_element_type=jnp.float32,
        )
        total = total + (term if factor is None else factor * term)
    total = total.astype(jnp.bfloat16)
    for v in range(VIS):
        for tile in range(PT):
            matched_ref[v * PT + tile] = total[
                tile * CH : (tile + 1) * CH, v * TILE : (v + 1) * TILE
            ]


def remote(src, dst, send, recv, visit, patch):
    return pltpu.make_async_remote_copy(
        src_ref=src,
        dst_ref=dst,
        send_sem=send,
        recv_sem=recv,
        device_id={"visit": visit, "patch": patch},
        device_id_type=MESH,
    )


def kernel(
    ids_ref, valid_ref, weights_ref, terms_ref, science_ref,
    prior_ref, prior_weight_ref, across_ref, down_ref, out_ref,
    w_ref, columns_ref, padded_ref, matched_ref, outgoing_ref, arrived_ref,
    back_0, back_1, back_2, back_3,
    acc_ref, give_ref, share_ref, edge_out, edge_ref, prior_vmem,
    slot_weight_vmem, terms_vmem, source_vmem, label_out, labels_vmem, coef_out, coefs_vmem,
    sum_out, sums_vmem,
    slot_weight_ref, kw_ref, source_ref, position_ref, labels_ref, coef_ref,
    local_sem, label_send, label_recv, coef_send, coef_recv, tile_send, tile_recv,
    share_send, share_recv, strip_send, strip_recv, edge_send, edge_recv,
    sum_send, sum_recv, back_send, back_recv,
):
    visit = lax.axis_index("visit")
    me = lax.axis_index("patch")
    own = visit
    returned = (back_0, back_1, back_2, back_3)
    slots = VIS * PT

    def peer(k):
        return lax.rem(me + k, OWNERS)

    def origin(k):
        return lax.rem(me + OWNERS - k, OWNERS)

    def other(k):
        return lax.rem(visit + k, VISITORS)

    def earlier(k):
        return lax.rem(visit + VISITORS - k, VISITORS)

    def neighbour(side):
        return peer(1) if side == 0 else origin(1)

    barrier = pltpu.get_barrier_semaphore()

    def greet(to_visit, to_patch):
        pl.semaphore_signal(
            barrier, inc=1, device_id={"visit": to_visit, "patch": to_patch}, device_id_type=MESH
        )

    @pl.loop(1, OWNERS)
    def _(k):
        greet(visit, peer(k))

    @pl.loop(1, VISITORS)
    def _(k):
        greet(other(k), me)
        greet(other(k), peer(1))
        greet(other(k), origin(1))

    prior_copies = [
        pltpu.make_async_copy(
            ref.at[pl.ds(pl.multiple_of(own * 256, 256), 256), :],
            prior_vmem.at[n],
            local_sem.at[n],
        )
        for n, ref in enumerate((prior_ref, prior_weight_ref))
    ]
    for copy in prior_copies:
        copy.start()
    slot_weight_vmem[...] = weights_ref[...].astype(jnp.float32)
    terms_vmem[...] = terms_ref[...].astype(jnp.float32)
    weight_copy = pltpu.make_async_copy(slot_weight_vmem, slot_weight_ref, local_sem.at[2])
    terms_copy = pltpu.make_async_copy(terms_vmem, kw_ref, local_sem.at[3])
    weight_copy.start()
    terms_copy.start()

    @pl.loop(0, slots)
    def _(n):
        strip = ids_ref[n // PT, n % PT] // PT
        rank = 0
        for m in range(slots):
            same = (ids_ref[m // PT, m % PT] // PT == strip) & (m < n)
            rank = rank + same.astype(jnp.int32)
        position_ref[n] = strip * CAP + rank

    lane = lax.broadcasted_iota(jnp.int32, (1, TILE), 1)
    source = jnp.zeros((1, TILE), jnp.int32)
    label = jnp.zeros((1, TILE), jnp.int32)
    for n in range(slots):
        here = lane == position_ref[n]
        source = jnp.where(here, n, source)
        label = jnp.where(here, n // PT * PT + ids_ref[n // PT, n % PT] % PT, label)
    source_vmem[...] = source
    label_out[...] = label
    source_copy = pltpu.make_async_copy(source_vmem, source_ref, local_sem.at[4])
    source_copy.start()
    weight_copy.wait()
    owner_row = lax.broadcasted_iota(jnp.int32, (OWNERS, TILE), 0)
    entry = lax.broadcasted_iota(jnp.int32, (OWNERS, TILE), 1)
    coefs = jnp.zeros((OWNERS, TILE), jnp.float32)
    for n in range(slots):
        v, s = n // PT, n % PT
        at = position_ref[n]
        here = (owner_row == at // CAP) & (entry == ids_ref[v, s] % PT * CAP + at % CAP)
        weight = slot_weight_ref[v, s] * valid_ref[v, s].astype(jnp.float32)
        coefs = jnp.where(here, weight, coefs)
    for to in range(OWNERS):
        coef_out[to] = coefs[to : to + 1]
    source_copy.wait()
    terms_copy.wait()

    pl.semaphore_wait(barrier, OWNERS - 1 + 3 * (VISITORS - 1))

    def coef_copy(k, to, slot):
        return remote(
            coef_out.at[to], coefs_vmem.at[slot], coef_send.at[k], coef_recv.at[slot], visit, to
        )

    def label_copy(k, to, slot):
        return remote(
            label_out, labels_vmem.at[slot], label_send.at[k], label_recv.at[slot], visit, to
        )

    def tile_copy(part, k, to, slot):
        return remote(
            outgoing_ref.at[part, to], arrived_ref.at[part, slot],
            tile_send.at[part, k], tile_recv.at[part, slot], visit, to,
        )

    def back_copy(part, k, to, slot):
        return remote(
            outgoing_ref.at[part, to], returned[part].at[slot],
            back_send.at[part, k], back_recv.at[part, slot], visit, to,
        )

    def sum_copy(k):
        return remote(sum_out, sums_vmem.at[k], sum_send.at[k], sum_recv.at[k], other(k), me)

    def share_copy(part, k):
        return remote(
            give_ref.at[part, other(k)], share_ref.at[part, k],
            share_send.at[part, k], share_recv.at[part, k], other(k), me,
        )

    def strip_copy(part, k, owner):
        rows = padded_ref.at[part, pl.ds(1 + 2 * owner, 2), :, pl.ds(0, TILE)]
        return remote(rows, rows, strip_send.at[part, k], strip_recv.at[part, k], other(k), me)

    def edge_copy(part, side, k):
        return remote(
            edge_out.at[part], edge_ref.at[part, side, k],
            edge_send.at[part, side, k], edge_recv.at[part, side, k], other(k), neighbour(side),
        )

    def pack(part, to, target, at):
        rows = pl.ds(pl.multiple_of(part * CH, 16), CH)
        for c in range(CAP):
            target[part, at, c] = science_ref[source_ref[0, to * CAP + c], rows, :]

    @pl.loop(1, OWNERS)
    def _(k):
        coef_copy(k, peer(k), me).start()

    @pl.loop(0, CHUNKS)
    def _(part):
        @pl.loop(1, OWNERS)
        def _(k):
            pack(part, peer(k), outgoing_ref, peer(k))
            tile_copy(part, k, peer(k), me).start()

        pack(part, me, arrived_ref, me)

    @pl.loop(1, OWNERS)
    def _(k):
        label_copy(k, peer(k), me).start()

    labels_vmem[me] = label_out[...]
    coefs_vmem[me] = coef_out[me]

    @pl.loop(1, OWNERS)
    def _(k):
        coef_copy(k, origin(k), origin(k)).wait_recv()

    coef_local = pltpu.make_async_copy(coefs_vmem, coef_ref, local_sem.at[5])
    coef_local.start()
    row = coefs_vmem[0]
    for at in range(1, OWNERS):
        row = row + coefs_vmem[at]
    sum_out[...] = row

    @pl.loop(1, VISITORS)
    def _(k):
        sum_copy(k).start()

    build_weights(me, kw_ref, across_ref, w_ref)
    blank = jnp.zeros((CH, 2 * TILE), jnp.bfloat16)
    for part in range(CHUNKS):
        padded_ref[part, 0] = blank
        padded_ref[part, PT + 1] = blank
    for copy in prior_copies:
        copy.wait()
    coef_local.wait()

    def add_slots(part, at, fresh):
        tiles = [arrived_ref[part, at, c].astype(jnp.float32) for c in range(CAP)]
        for t in range(PT):
            value = None if fresh else acc_ref[t]
            for c in range(CAP):
                term = coef_ref[at, 0, t * CAP + c] * tiles[c]
                value = term if value is None else value + term
            acc_ref[t] = value

    def gather(part):
        add_slots(part, me, True)

        @pl.loop(1, OWNERS)
        def _(k):
            at = origin(k)
            tile_copy(part, k, at, at).wait_recv()
            add_slots(part, at, False)

        for to in range(VISITORS):
            for n in range(2):
                give_ref[part, to, n] = acc_ref[2 * to + n].astype(jnp.bfloat16)

        @pl.loop(1, VISITORS)
        def _(k):
            share_copy(part, k).start()

    def finish(part):
        @pl.loop(1, VISITORS)
        def _(k):
            share_copy(part, k).wait_recv()

        total_row = sum_out[...]
        for k in range(1, VISITORS):
            total_row = total_row + sums_vmem[k]
        spot = lax.broadcasted_iota(jnp.int32, (HALO, TILE), 1)
        packed = jnp.zeros((HALO, TILE), jnp.float32)
        for n in range(2):
            total = acc_ref[own * 2 + n]
            for k in range(1, VISITORS):
                total = total + share_ref[part, k, n].astype(jnp.float32)
            weight_sum = jnp.sum(
                jnp.where(lane // CAP == own * 2 + n, total_row, 0.0), axis=1, keepdims=True
            )
            rows = pl.ds(pl.multiple_of(n * TILE + part * CH, 16), CH)
            weight = prior_vmem[1, rows, :]
            template = (weight * prior_vmem[0, rows, :] + total) / (weight + weight_sum)
            template = template.astype(jnp.bfloat16)
            padded_ref[part, 1 + own * 2 + n, :, :TILE] = template
            wide = template.astype(jnp.float32)
            for h in range(2):
                g = 2 * n + h
                moved = pltpu.roll(
                    wide[h * HALO : (h + 1) * HALO], (2 * HALO * g + HALO) % TILE, 1
                )
                packed = jnp.where(spot // (2 * HALO) == g, moved, packed)
        edge_out[part] = packed.astype(jnp.bfloat16)

        @pl.loop(0, VISITORS)
        def _(k):
            for side in range(2):
                edge_copy(part, side, k).start()

        @pl.loop(1, VISITORS)
        def _(k):
            strip_copy(part, k, own).start()

    def wait_strips(part):
        spot = lax.broadcasted_iota(jnp.int32, (HALO, TILE), 1)

        @pl.loop(1, VISITORS)
        def _(k):
            strip_copy(part, k, earlier(k)).wait_recv()

        @pl.loop(0, VISITORS)
        def _(k):
            for side in range(2):
                edge_copy(part, side, k).wait_recv()
            left = jnp.where(me > 0, edge_ref[part, 0, k].astype(jnp.float32), 0.0)
            right = jnp.where(me < OWNERS - 1, edge_ref[part, 1, k].astype(jnp.float32), 0.0)
            both = jnp.where(spot % (2 * HALO) < HALO, left, right)
            for g in range(4):
                moved = pltpu.roll(both, (TILE - 2 * HALO * g) % TILE, 1) if g else both
                moved = jnp.where(spot < 2 * HALO, moved, 0.0).astype(jnp.bfloat16)
                n, h = g // 2, g % 2
                padded_ref[
                    part, 1 + earlier(k) * 2 + n, h * HALO : (h + 1) * HALO, TILE:
                ] = moved

    @pl.loop(0, CHUNKS)
    def _(step):
        gather(step)

        @pl.when(step == 0)
        def _():
            @pl.loop(1, VISITORS)
            def _(k):
                sum_copy(k).wait_recv()

        @pl.when(step < CHUNKS - 1)
        def _():
            finish(step)

    @pl.loop(1, OWNERS)
    def _(k):
        label_copy(k, origin(k), origin(k)).wait_recv()

    label_local = pltpu.make_async_copy(labels_vmem, labels_ref, local_sem.at[6])
    label_local.start()

    @pl.loop(0, CHUNKS)
    def _(part):
        @pl.loop(1, OWNERS)
        def _(k):
            tile_copy(part, k, peer(k), me).wait_send()

    @pl.loop(0, CHUNKS - 1)
    def _(part):
        wait_strips(part)

    label_local.wait()

    @pl.loop(0, CHUNKS)
    def _(step):
        part = lax.rem(step + 1, CHUNKS)

        @pl.when(step == 1)
        def _():
            wait_strips(CHUNKS - 1)

        match_chunk(part, padded_ref, down_ref, w_ref, columns_ref, matched_ref)

        @pl.when(step == 0)
        def _():
            finish(CHUNKS - 1)

        @pl.loop(1, OWNERS)
        def _(k):
            to = peer(k)
            for c in range(CAP):
                outgoing_ref[part, to, c] = matched_ref[labels_ref[to, 0, me * CAP + c]]
            for q in range(CHUNKS):

                @pl.when(part == q)
                def _():
                    back_copy(q, k, to, me).start()

        for q in range(CHUNKS):

            @pl.when(part == q)
            def _():
                for c in range(CAP):
                    returned[q][me, c] = matched_ref[labels_ref[me, 0, me * CAP + c]]

    for step in range(CHUNKS):
        part = (step + 1) % CHUNKS
        rows = pl.ds(part * CH, CH)

        @pl.loop(1, OWNERS)
        def _(k):
            back_copy(part, k, origin(k), origin(k)).wait_recv()

        @pl.loop(0, slots)
        def _(n):
            at = position_ref[n]
            matched = returned[part][at // CAP, at % CAP].astype(jnp.float32)
            value = science_ref[n, rows, :].astype(jnp.float32) - matched
            keep = valid_ref[n // PT, n % PT].astype(jnp.float32)
            out_ref[n, rows, :] = (value * keep).astype(jnp.bfloat16)

    @pl.loop(1, OWNERS)
    def _(k):
        coef_copy(k, peer(k), me).wait_send()
        label_copy(k, peer(k), me).wait_send()

    @pl.loop(1, VISITORS)
    def _(k):
        sum_copy(k).wait_send()

    @pl.loop(0, CHUNKS)
    def _(part):
        @pl.loop(1, VISITORS)
        def _(k):
            share_copy(part, k).wait_send()
            strip_copy(part, k, own).wait_send()

        @pl.loop(0, VISITORS)
        def _(k):
            for side in range(2):
                edge_copy(part, side, k).wait_send()

    for part in range(CHUNKS):

        @pl.loop(1, OWNERS)
        def _(k):
            back_copy(part, k, peer(k), me).wait_send()


def body(science, tile_ids, valid, weights, kernel_weight_terms, prior_template, prior_weight):
    slots = tile_ids.size
    across, down = band_constants()
    vmem = pl.BlockSpec(memory_space=pltpu.VMEM)
    smem = pl.BlockSpec(memory_space=pltpu.SMEM)
    hbm = pl.BlockSpec(memory_space=pl.ANY)
    dma = pltpu.SemaphoreType.DMA
    f32, bf16, i32 = jnp.float32, jnp.bfloat16, jnp.int32
    result = pl.pallas_call(
        kernel,
        out_shape=jax.ShapeDtypeStruct((slots, TILE, TILE), jnp.bfloat16),
        in_specs=[smem, smem, vmem, vmem, vmem, hbm, hbm, vmem, vmem],
        out_specs=vmem,
        scratch_shapes=[
            pltpu.VMEM((DEEP, GROUP), bf16),
            pltpu.VMEM((PT * CH, DEEP), bf16),
            pltpu.VMEM((CHUNKS, PT + 2, CH, 2 * TILE), bf16),
            pltpu.VMEM((VIS * PT, CH, TILE), bf16),
            pltpu.VMEM((CHUNKS, OWNERS, CAP, CH, TILE), bf16),
            pltpu.VMEM((CHUNKS, OWNERS, CAP, CH, TILE), bf16),
            pltpu.VMEM((OWNERS, CAP, CH, TILE), bf16),
            pltpu.VMEM((OWNERS, CAP, CH, TILE), bf16),
            pltpu.VMEM((OWNERS, CAP, CH, TILE), bf16),
            pltpu.VMEM((OWNERS, CAP, CH, TILE), bf16),
            pltpu.VMEM((PT, CH, TILE), f32),
            pltpu.VMEM((CHUNKS, VISITORS, 2, CH, TILE), bf16),
            pltpu.VMEM((CHUNKS, VISITORS, 2, CH, TILE), bf16),
            pltpu.VMEM((CHUNKS, HALO, TILE), bf16),
            pltpu.VMEM((CHUNKS, 2, VISITORS, HALO, TILE), bf16),
            pltpu.VMEM((2, 2 * TILE, TILE), f32),
            pltpu.VMEM(weights.shape, f32),
            pltpu.VMEM(kernel_weight_terms.shape, f32),
            pltpu.VMEM((1, TILE), i32),
            pltpu.VMEM((1, TILE), i32),
            pltpu.VMEM((OWNERS, 1, TILE), i32),
            pltpu.VMEM((OWNERS, 1, TILE), f32),
            pltpu.VMEM((OWNERS, 1, TILE), f32),
            pltpu.VMEM((1, TILE), f32),
            pltpu.VMEM((VISITORS, 1, TILE), f32),
            pltpu.SMEM(weights.shape, f32),
            pltpu.SMEM(kernel_weight_terms.shape, f32),
            pltpu.SMEM((1, TILE), i32),
            pltpu.SMEM((slots,), i32),
            pltpu.SMEM((OWNERS, 1, TILE), i32),
            pltpu.SMEM((OWNERS, 1, TILE), f32),
            dma((7,)),
            dma((OWNERS,)),
            dma((OWNERS,)),
            dma((OWNERS,)),
            dma((OWNERS,)),
            dma((CHUNKS, OWNERS)),
            dma((CHUNKS, OWNERS)),
            dma((CHUNKS, VISITORS)),
            dma((CHUNKS, VISITORS)),
            dma((CHUNKS, VISITORS)),
            dma((CHUNKS, VISITORS)),
            dma((CHUNKS, 2, VISITORS)),
            dma((CHUNKS, 2, VISITORS)),
            dma((VISITORS,)),
            dma((VISITORS,)),
            dma((CHUNKS, OWNERS)),
            dma((CHUNKS, OWNERS)),
        ],
        compiler_params=pltpu.CompilerParams(
            vmem_limit_bytes=56 << 20, collective_id=0, has_side_effects=True
        ),
    )(
        tile_ids,
        valid,
        weights,
        kernel_weight_terms,
        science.reshape(slots, TILE, TILE),
        prior_template,
        prior_weight,
        jnp.asarray(across),
        jnp.asarray(down),
    )
    return result.reshape(science.shape)


def solution(mesh):
    placed = (
        P("visit", "patch", None, None),
        P("visit", "patch"),
        P("visit", "patch"),
        P("visit", "patch"),
        P("visit", None, None),
        P(None, "patch"),
        P(None, "patch"),
    )
    return jax.shard_map(
        body, mesh=mesh, in_specs=placed, out_specs=P("visit", "patch", None, None), check_vma=False
    )
```

time: 95.6 us -> 92.5 us (0.968); the launches traced: 95.4 us -> 91.2 us
  local copies, waits for them, and re-layouts: 6.43 us -> 3.59 us
  other arithmetic: 1.52 us -> 0 us
    pad x2 -> x0, local copies, waits for them, and re-layouts: 1.22 us -> none  [the longest x1 0.62 us: body(): jnp.pad(weight, spread)]
    unnamed x13 -> x2, local copies, waits for them, and re-layouts: 4.81 us -> 3.59 us
where the time goes in v3:
time: 92.5 us; the launch traced here: 91.2 us
  Pallas kernels  87.6 us (95%)
  local copies, waits for them, and re-layouts  3.59 us (4%)
    pallas_call x1, Pallas kernels, body(): pl.pallas_call(kernel, out_shape=jax.ShapeDtypeStruct((slots, TILE, TILE)...  87.6 us
    unnamed x2, local copies, waits for them, and re-layouts  3.59 us

profile of v3, /device:TPU:0, one launch (start us, length us, event | category | flops | bytes accessed | tf_op | source)
XLA Modules:
  0.0 91.2 jit_solution(11767615307683653441)
XLA Ops:
  0.0 1.3 %copy.10.terms_ref = bf16[2,6,25]{2,1,0:T(8,128)(2,1)} copy(bf16[2,6,25]{2,0,1:T(2,128)(2,1)} %param.13) | data formatting | bytes 1200 | tf_op args[4]
  1.3 87.6 %shard_map.91 = bf16[32,128,128]{2,1,0:T(8,128)(2,1)} custom-call(s32[2,16]{1,0:T(2,128)} %ids_ref.1, s32[2,16]{1,0:T(2,128)} %valid_ref.1, bf16[2,16]{1,0:T(2,128)(2,1)} %weights_ref.1, bf16[2,6,25]{2,1,0:T(8,128)(2,1)} %copy.10.terms_ref, bf16[32,128,128]{2,1,0:T(8,128)(2,1)} %bitcast.3, f32[2048,128]{1,0:T(8,128)} %prior_ref.1, ...), custom_call_target="tpu_custom_call" | custom-call | tf_op jit(solution)/shard_map/pallas_call | solution.py:559
  88.9 2.3 %copy.12 = bf16[2,16,128,128]{3,2,1,0:T(8,128)(2,1)} copy(bf16[2,16,128,128]{3,2,1,0:T(8,128)(2,1)} %bitcast.2) | data formatting | bytes 2097152

commit v4 on v3

--- a/solution.py
+++ b/solution.py
@@ -22,6 +22,7 @@
 GROUP = 3 * VIS * TILE
 CH = 32
 CHUNKS = TILE // CH
+GATHERED = 5
 MAIN = NPROF * TILE
 DEEP = MAIN + 3 * TILE
 OWNERS = 16
@@ -80,7 +81,7 @@
         for v in range(VIS):
             sums = [None, None, None]
             for n, source in enumerate(sources):
-                c = [kw_ref[v, m, k + n] for m in range(NPOLY)]
+                c = [kw_ref[m, v, k + n] for m in range(NPOLY)]
                 rows = (c[0] + c[1] * x + c[3] * xx, c[2] + c[4] * x, c[5])
                 image = across_ref[source].astype(jnp.float32)
                 for b in range(3):
@@ -127,7 +128,7 @@
 
     half = VIS * TILE
     line = lax.broadcasted_iota(jnp.int32, (PT * CH, 1), 0)
-    y = (line // CH * TILE + part * CH + line % CH).astype(jnp.float32)
+    y = ((line >> 5) * TILE + part * CH + (line & (CH - 1))).astype(jnp.float32)
     y = (y + 0.5) / SKY * 2.0 - 1.0
     total = jnp.zeros((PT * CH, half), jnp.float32)
     for power, factor in enumerate((None, y, y * y)):
@@ -157,11 +158,12 @@
 
 
 def kernel(
-    ids_ref, valid_ref, weights_ref, terms_ref, science_ref,
-    prior_ref, prior_weight_ref, across_ref, down_ref, out_ref,
+    ids_ref, valid_ref, weights_ref, terms_ref, science_hbm,
+    prior_ref, prior_weight_ref, across_hbm, down_hbm, out_ref,
+    out_vmem, science_ref, across_ref, down_ref,
     w_ref, columns_ref, padded_ref, matched_ref, outgoing_ref, arrived_ref,
     back_0, back_1, back_2, back_3,
-    acc_ref, give_ref, share_ref, edge_out, edge_ref, prior_vmem,
+    back_out, acc_ref, own_ref, give_ref, share_ref, edge_out, edge_ref, prior_vmem,
     slot_weight_vmem, terms_vmem, source_vmem, label_out, labels_vmem, coef_out, coefs_vmem,
     sum_out, sums_vmem,
     slot_weight_ref, kw_ref, source_ref, position_ref, labels_ref, coef_ref,
@@ -190,6 +192,10 @@
     def neighbour(side):
         return peer(1) if side == 0 else origin(1)
 
+    science_copy = pltpu.make_async_copy(science_hbm, science_ref, local_sem.at[7])
+    across_copy = pltpu.make_async_copy(across_hbm, across_ref, local_sem.at[8])
+    down_copy = pltpu.make_async_copy(down_hbm, down_ref, local_sem.at[9])
+    science_copy.start()
     barrier = pltpu.get_barrier_semaphore()
 
     def greet(to_visit, to_patch):
@@ -217,6 +223,8 @@
     ]
     for copy in prior_copies:
         copy.start()
+    across_copy.start()
+    down_copy.start()
     slot_weight_vmem[...] = weights_ref[...].astype(jnp.float32)
     terms_vmem[...] = terms_ref[...].astype(jnp.float32)
     weight_copy = pltpu.make_async_copy(slot_weight_vmem, slot_weight_ref, local_sem.at[2])
@@ -224,14 +232,14 @@
     weight_copy.start()
     terms_copy.start()
 
-    @pl.loop(0, slots)
-    def _(n):
-        strip = ids_ref[n // PT, n % PT] // PT
+    ids = [ids_ref[n // PT, n % PT] for n in range(slots)]
+    strips = [value >> 4 for value in ids]
+    tiles = [value & (PT - 1) for value in ids]
+    for n in range(slots):
         rank = 0
-        for m in range(slots):
-            same = (ids_ref[m // PT, m % PT] // PT == strip) & (m < n)
-            rank = rank + same.astype(jnp.int32)
-        position_ref[n] = strip * CAP + rank
+        for m in range(n):
+            rank = rank + jnp.where(strips[m] == strips[n], 1, 0)
+        position_ref[n] = strips[n] * CAP + rank
 
     lane = lax.broadcasted_iota(jnp.int32, (1, TILE), 1)
     source = jnp.zeros((1, TILE), jnp.int32)
@@ -239,7 +247,7 @@
     for n in range(slots):
         here = lane == position_ref[n]
         source = jnp.where(here, n, source)
-        label = jnp.where(here, n // PT * PT + ids_ref[n // PT, n % PT] % PT, label)
+        label = jnp.where(here, n // PT * PT + tiles[n], label)
     source_vmem[...] = source
     label_out[...] = label
     source_copy = pltpu.make_async_copy(source_vmem, source_ref, local_sem.at[4])
@@ -251,55 +259,62 @@
     for n in range(slots):
         v, s = n // PT, n % PT
         at = position_ref[n]
-        here = (owner_row == at // CAP) & (entry == ids_ref[v, s] % PT * CAP + at % CAP)
+        here = (owner_row == at >> 2) & (entry == tiles[n] * CAP + (at & (CAP - 1)))
         weight = slot_weight_ref[v, s] * valid_ref[v, s].astype(jnp.float32)
         coefs = jnp.where(here, weight, coefs)
     for to in range(OWNERS):
         coef_out[to] = coefs[to : to + 1]
     source_copy.wait()
     terms_copy.wait()
+    science_copy.wait()
 
     pl.semaphore_wait(barrier, OWNERS - 1 + 3 * (VISITORS - 1))
 
     def coef_copy(k, to, slot):
         return remote(
-            coef_out.at[to], coefs_vmem.at[slot], coef_send.at[k], coef_recv.at[slot], visit, to
+            coef_out.at[to], coefs_vmem.at[slot], coef_send, coef_recv, visit, to
         )
 
     def label_copy(k, to, slot):
         return remote(
-            label_out, labels_vmem.at[slot], label_send.at[k], label_recv.at[slot], visit, to
+            label_out, labels_vmem.at[slot], label_send, label_recv, visit, to
         )
 
     def tile_copy(part, k, to, slot):
         return remote(
             outgoing_ref.at[part, to], arrived_ref.at[part, slot],
-            tile_send.at[part, k], tile_recv.at[part, slot], visit, to,
+            tile_send, tile_recv.at[part, (k - 1) // GATHERED], visit, to,
         )
 
     def back_copy(part, k, to, slot):
         return remote(
-            outgoing_ref.at[part, to], returned[part].at[slot],
-            back_send.at[part, k], back_recv.at[part, slot], visit, to,
-        )
+            back_out.at[part, to], returned[part].at[slot],
+            back_send, back_recv.at[part], visit, to,
+        )
+
+    def arrive(block, semaphore):
+        remote(block, block, semaphore, semaphore, visit, peer(1)).wait_recv()
+
+    def leave(block, semaphore):
+        remote(block, block, semaphore, semaphore, visit, peer(1)).wait_send()
 
     def sum_copy(k):
-        return remote(sum_out, sums_vmem.at[k], sum_send.at[k], sum_recv.at[k], other(k), me)
+        return remote(sum_out, sums_vmem.at[k], sum_send, sum_recv, other(k), me)
 
     def share_copy(part, k):
         return remote(
             give_ref.at[part, other(k)], share_ref.at[part, k],
-            share_send.at[part, k], share_recv.at[part, k], other(k), me,
+            share_send, share_recv.at[part], other(k), me,
         )
 
     def strip_copy(part, k, owner):
         rows = padded_ref.at[part, pl.ds(1 + 2 * owner, 2), :, pl.ds(0, TILE)]
-        return remote(rows, rows, strip_send.at[part, k], strip_recv.at[part, k], other(k), me)
+        return remote(rows, rows, strip_send, strip_recv.at[part], other(k), me)
 
     def edge_copy(part, side, k):
         return remote(
             edge_out.at[part], edge_ref.at[part, side, k],
-            edge_send.at[part, side, k], edge_recv.at[part, side, k], other(k), neighbour(side),
+            edge_send, edge_recv.at[part], other(k), neighbour(side),
         )
 
     def pack(part, to, target, at):
@@ -310,6 +325,7 @@
     @pl.loop(1, OWNERS)
     def _(k):
         coef_copy(k, peer(k), me).start()
+        label_copy(k, peer(k), me).start()
 
     @pl.loop(0, CHUNKS)
     def _(part):
@@ -320,16 +336,10 @@
 
         pack(part, me, arrived_ref, me)
 
-    @pl.loop(1, OWNERS)
-    def _(k):
-        label_copy(k, peer(k), me).start()
-
     labels_vmem[me] = label_out[...]
     coefs_vmem[me] = coef_out[me]
 
-    @pl.loop(1, OWNERS)
-    def _(k):
-        coef_copy(k, origin(k), origin(k)).wait_recv()
+    arrive(coefs_vmem.at[pl.ds(0, OWNERS - 1)], coef_recv)
 
     coef_local = pltpu.make_async_copy(coefs_vmem, coef_ref, local_sem.at[5])
     coef_local.start()
@@ -342,6 +352,8 @@
     def _(k):
         sum_copy(k).start()
 
+    across_copy.wait()
+    down_copy.wait()
     build_weights(me, kw_ref, across_ref, w_ref)
     blank = jnp.zeros((CH, 2 * TILE), jnp.bfloat16)
     for part in range(CHUNKS):
@@ -363,11 +375,13 @@
     def gather(part):
         add_slots(part, me, True)
 
-        @pl.loop(1, OWNERS)
-        def _(k):
-            at = origin(k)
-            tile_copy(part, k, at, at).wait_recv()
-            add_slots(part, at, False)
+        @pl.loop(0, (OWNERS - 1) // GATHERED)
+        def _(group):
+            arrive(arrived_ref.at[part, pl.ds(0, GATHERED)], tile_recv.at[part, group])
+
+            @pl.loop(1, GATHERED + 1)
+            def _(k):
+                add_slots(part, origin(group * GATHERED + k), False)
 
         for to in range(VISITORS):
             for n in range(2):
@@ -377,10 +391,10 @@
         def _(k):
             share_copy(part, k).start()
 
+        own_ref[part] = acc_ref[pl.ds(own * 2, 2)]
+
     def finish(part):
-        @pl.loop(1, VISITORS)
-        def _(k):
-            share_copy(part, k).wait_recv()
+        arrive(share_ref.at[part, pl.ds(1, VISITORS - 1)], share_recv.at[part])
 
         total_row = sum_out[...]
         for k in range(1, VISITORS):
@@ -388,11 +402,11 @@
         spot = lax.broadcasted_iota(jnp.int32, (HALO, TILE), 1)
         packed = jnp.zeros((HALO, TILE), jnp.float32)
         for n in range(2):
-            total = acc_ref[own * 2 + n]
+            total = own_ref[part, n]
             for k in range(1, VISITORS):
                 total = total + share_ref[part, k, n].astype(jnp.float32)
             weight_sum = jnp.sum(
-                jnp.where(lane // CAP == own * 2 + n, total_row, 0.0), axis=1, keepdims=True
+                jnp.where(lane >> 2 == own * 2 + n, total_row, 0.0), axis=1, keepdims=True
             )
             rows = pl.ds(pl.multiple_of(n * TILE + part * CH, 16), CH)
             weight = prior_vmem[1, rows, :]
@@ -405,7 +419,7 @@
                 moved = pltpu.roll(
                     wide[h * HALO : (h + 1) * HALO], (2 * HALO * g + HALO) % TILE, 1
                 )
-                packed = jnp.where(spot // (2 * HALO) == g, moved, packed)
+                packed = jnp.where(spot >> 5 == g, moved, packed)
         edge_out[part] = packed.astype(jnp.bfloat16)
 
         @pl.loop(0, VISITORS)
@@ -420,17 +434,16 @@
     def wait_strips(part):
         spot = lax.broadcasted_iota(jnp.int32, (HALO, TILE), 1)
 
-        @pl.loop(1, VISITORS)
-        def _(k):
-            strip_copy(part, k, earlier(k)).wait_recv()
+        arrive(
+            padded_ref.at[part, pl.ds(1, PT - 2), :, pl.ds(0, TILE)], strip_recv.at[part]
+        )
+        arrive(edge_ref.at[part], edge_recv.at[part])
 
         @pl.loop(0, VISITORS)
         def _(k):
-            for side in range(2):
-                edge_copy(part, side, k).wait_recv()
             left = jnp.where(me > 0, edge_ref[part, 0, k].astype(jnp.float32), 0.0)
             right = jnp.where(me < OWNERS - 1, edge_ref[part, 1, k].astype(jnp.float32), 0.0)
-            both = jnp.where(spot % (2 * HALO) < HALO, left, right)
+            both = jnp.where(spot & (2 * HALO - 1) < HALO, left, right)
             for g in range(4):
                 moved = pltpu.roll(both, (TILE - 2 * HALO * g) % TILE, 1) if g else both
                 moved = jnp.where(spot < 2 * HALO, moved, 0.0).astype(jnp.bfloat16)
@@ -439,38 +452,36 @@
                     part, 1 + earlier(k) * 2 + n, h * HALO : (h + 1) * HALO, TILE:
                 ] = moved
 
-    @pl.loop(0, CHUNKS)
+    label_local = pltpu.make_async_copy(labels_vmem, labels_ref, local_sem.at[6])
+
+    @pl.loop(0, CHUNKS - 1)
     def _(step):
         gather(step)
 
+        @pl.when(step == 1)
+        def _():
+            arrive(labels_vmem.at[pl.ds(0, OWNERS - 1)], label_recv)
+            label_local.start()
+            label_local.wait()
+
         @pl.when(step == 0)
         def _():
-            @pl.loop(1, VISITORS)
-            def _(k):
-                sum_copy(k).wait_recv()
-
-        @pl.when(step < CHUNKS - 1)
+            arrive(sums_vmem.at[pl.ds(1, VISITORS - 1)], sum_recv)
+
+        @pl.when(step > 0)
         def _():
-            finish(step)
-
-    @pl.loop(1, OWNERS)
-    def _(k):
-        label_copy(k, origin(k), origin(k)).wait_recv()
-
-    label_local = pltpu.make_async_copy(labels_vmem, labels_ref, local_sem.at[6])
-    label_local.start()
-
-    @pl.loop(0, CHUNKS)
-    def _(part):
-        @pl.loop(1, OWNERS)
-        def _(k):
-            tile_copy(part, k, peer(k), me).wait_send()
-
-    @pl.loop(0, CHUNKS - 1)
+            finish(step - 1)
+
+        @pl.when(step > 1)
+        def _():
+            wait_strips(step - 2)
+
+    finish(CHUNKS - 2)
+    gather(CHUNKS - 1)
+
+    @pl.loop(CHUNKS - 3, CHUNKS - 1)
     def _(part):
         wait_strips(part)
-
-    label_local.wait()
 
     @pl.loop(0, CHUNKS)
     def _(step):
@@ -490,7 +501,7 @@
         def _(k):
             to = peer(k)
             for c in range(CAP):
-                outgoing_ref[part, to, c] = matched_ref[labels_ref[to, 0, me * CAP + c]]
+                back_out[part, to, c] = matched_ref[labels_ref[to, 0, me * CAP + c]]
             for q in range(CHUNKS):
 
                 @pl.when(part == q)
@@ -504,48 +515,36 @@
                 for c in range(CAP):
                     returned[q][me, c] = matched_ref[labels_ref[me, 0, me * CAP + c]]
 
+    written = []
     for step in range(CHUNKS):
         part = (step + 1) % CHUNKS
         rows = pl.ds(part * CH, CH)
-
-        @pl.loop(1, OWNERS)
-        def _(k):
-            back_copy(part, k, origin(k), origin(k)).wait_recv()
+        arrive(returned[part].at[pl.ds(0, OWNERS - 1)], back_recv.at[part])
 
         @pl.loop(0, slots)
         def _(n):
             at = position_ref[n]
-            matched = returned[part][at // CAP, at % CAP].astype(jnp.float32)
+            matched = returned[part][at >> 2, at & (CAP - 1)].astype(jnp.float32)
             value = science_ref[n, rows, :].astype(jnp.float32) - matched
             keep = valid_ref[n // PT, n % PT].astype(jnp.float32)
-            out_ref[n, rows, :] = (value * keep).astype(jnp.bfloat16)
-
-    @pl.loop(1, OWNERS)
-    def _(k):
-        coef_copy(k, peer(k), me).wait_send()
-        label_copy(k, peer(k), me).wait_send()
-
-    @pl.loop(1, VISITORS)
-    def _(k):
-        sum_copy(k).wait_send()
-
-    @pl.loop(0, CHUNKS)
-    def _(part):
-        @pl.loop(1, VISITORS)
-        def _(k):
-            share_copy(part, k).wait_send()
-            strip_copy(part, k, own).wait_send()
-
-        @pl.loop(0, VISITORS)
-        def _(k):
-            for side in range(2):
-                edge_copy(part, side, k).wait_send()
-
-    for part in range(CHUNKS):
-
-        @pl.loop(1, OWNERS)
-        def _(k):
-            back_copy(part, k, peer(k), me).wait_send()
+            out_vmem[n, rows, :] = (value * keep).astype(jnp.bfloat16)
+
+        copy = pltpu.make_async_copy(
+            out_vmem.at[:, rows, :], out_ref.at[:, rows, :], local_sem.at[10 + part]
+        )
+        copy.start()
+        written.append(copy)
+
+    leave(coefs_vmem.at[pl.ds(0, OWNERS - 1)], coef_send)
+    leave(labels_vmem.at[pl.ds(0, OWNERS - 1)], label_send)
+    leave(sums_vmem.at[pl.ds(1, VISITORS - 1)], sum_send)
+    leave(give_ref.at[:, pl.ds(0, VISITORS - 1)], share_send)
+    leave(padded_ref.at[:, pl.ds(1, PT - 2), :, pl.ds(0, TILE)], strip_send)
+    leave(edge_ref, edge_send)
+    leave(outgoing_ref.at[:, pl.ds(0, OWNERS - 1)], tile_send)
+    leave(back_out.at[:, pl.ds(0, OWNERS - 1)], back_send)
+    for copy in written:
+        copy.wait()
 
 
 def body(science, tile_ids, valid, weights, kernel_weight_terms, prior_template, prior_weight):
@@ -559,9 +558,13 @@
     result = pl.pallas_call(
         kernel,
         out_shape=jax.ShapeDtypeStruct((slots, TILE, TILE), jnp.bfloat16),
-        in_specs=[smem, smem, vmem, vmem, vmem, hbm, hbm, vmem, vmem],
-        out_specs=vmem,
+        in_specs=[smem, smem, vmem, vmem, hbm, hbm, hbm, hbm, hbm],
+        out_specs=hbm,
         scratch_shapes=[
+            pltpu.VMEM((slots, TILE, TILE), bf16),
+            pltpu.VMEM((slots, TILE, TILE), bf16),
+            pltpu.VMEM(across.shape, bf16),
+            pltpu.VMEM(down.shape, bf16),
             pltpu.VMEM((DEEP, GROUP), bf16),
             pltpu.VMEM((PT * CH, DEEP), bf16),
             pltpu.VMEM((CHUNKS, PT + 2, CH, 2 * TILE), bf16),
@@ -572,14 +575,16 @@
             pltpu.VMEM((OWNERS, CAP, CH, TILE), bf16),
             pltpu.VMEM((OWNERS, CAP, CH, TILE), bf16),
             pltpu.VMEM((OWNERS, CAP, CH, TILE), bf16),
+            pltpu.VMEM((CHUNKS, OWNERS, CAP, CH, TILE), bf16),
             pltpu.VMEM((PT, CH, TILE), f32),
+            pltpu.VMEM((CHUNKS, 2, CH, TILE), f32),
             pltpu.VMEM((CHUNKS, VISITORS, 2, CH, TILE), bf16),
             pltpu.VMEM((CHUNKS, VISITORS, 2, CH, TILE), bf16),
             pltpu.VMEM((CHUNKS, HALO, TILE), bf16),
             pltpu.VMEM((CHUNKS, 2, VISITORS, HALO, TILE), bf16),
             pltpu.VMEM((2, 2 * TILE, TILE), f32),
             pltpu.VMEM(weights.shape, f32),
-            pltpu.VMEM(kernel_weight_terms.shape, f32),
+            pltpu.VMEM((NPOLY, VIS, NBASIS), f32),
             pltpu.VMEM((1, TILE), i32),
             pltpu.VMEM((1, TILE), i32),
             pltpu.VMEM((OWNERS, 1, TILE), i32),
@@ -588,28 +593,28 @@
             pltpu.VMEM((1, TILE), f32),
             pltpu.VMEM((VISITORS, 1, TILE), f32),
             pltpu.SMEM(weights.shape, f32),
-            pltpu.SMEM(kernel_weight_terms.shape, f32),
+            pltpu.SMEM((NPOLY, VIS, NBASIS), f32),
             pltpu.SMEM((1, TILE), i32),
             pltpu.SMEM((slots,), i32),
             pltpu.SMEM((OWNERS, 1, TILE), i32),
             pltpu.SMEM((OWNERS, 1, TILE), f32),
-            dma((7,)),
-            dma((OWNERS,)),
-            dma((OWNERS,)),
-            dma((OWNERS,)),
-            dma((OWNERS,)),
-            dma((CHUNKS, OWNERS)),
-            dma((CHUNKS, OWNERS)),
-            dma((CHUNKS, VISITORS)),
-            dma((CHUNKS, VISITORS)),
-            dma((CHUNKS, VISITORS)),
-            dma((CHUNKS, VISITORS)),
-            dma((CHUNKS, 2, VISITORS)),
-            dma((CHUNKS, 2, VISITORS)),
-            dma((VISITORS,)),
-            dma((VISITORS,)),
-            dma((CHUNKS, OWNERS)),
-            dma((CHUNKS, OWNERS)),
+            dma((10 + CHUNKS,)),
+            dma(()),
+            dma(()),
+            dma(()),
+            dma(()),
+            dma(()),
+            dma((CHUNKS, (OWNERS - 1) // GATHERED)),
+            dma(()),
+            dma((CHUNKS,)),
+            dma(()),
+            dma((CHUNKS,)),
+            dma(()),
+            dma((CHUNKS,)),
+            dma(()),
+            dma(()),
+            dma(()),
+            dma((CHUNKS,)),
         ],
         compiler_params=pltpu.CompilerParams(
             vmem_limit_bytes=56 << 20, collective_id=0, has_side_effects=True
@@ -618,7 +623,7 @@
         tile_ids,
         valid,
         weights,
-        kernel_weight_terms,
+        jnp.transpose(kernel_weight_terms, (1, 0, 2)),
         science.reshape(slots, TILE, TILE),
         prior_template,
         prior_weight,

time: 92.5 us -> 82.1 us (0.89)
  Pallas kernels: 87.6 us -> 78.7 us
  local copies, waits for them, and re-layouts: 3.59 us -> 2.31 us
    pallas_call x1, Pallas kernels: 87.6 us -> 78.7 us  [body(): pl.pallas_call(kernel, out_shape=jax.ShapeDtypeStruct((slots, TILE, TILE)...]
    unnamed x2 -> x1, local copies, waits for them, and re-layouts: 3.59 us -> 2.31 us
where the time goes in v4:
time: 82.1 us; the launch traced here: 81 us
  Pallas kernels  78.7 us (96%)
  local copies, waits for them, and re-layouts  2.31 us (3%)
    pallas_call x1, Pallas kernels, body(): pl.pallas_call(kernel, out_shape=jax.ShapeDtypeStruct((slots, TILE, TILE)...  78.7 us
    unnamed x1, local copies, waits for them, and re-layouts  2.31 us

profile of v4, /device:TPU:0, one launch (start us, length us, event | category | flops | bytes accessed | tf_op | source)
XLA Modules:
  0.0 81.0 jit_solution(14354148562935891603)
XLA Ops:
  0.0 78.7 %shard_map.91 = bf16[32,128,128]{2,1,0:T(8,128)(2,1)} custom-call(s32[2,16]{1,0:T(2,128)} %ids_ref.1, s32[2,16]{1,0:T(2,128)} %valid_ref.1, bf16[2,16]{1,0:T(2,128)(2,1)} %weights_ref.1, bf16[6,2,25]{2,1,0:T(2,128)(2,1)} %bitcast.5, bf16[32,128,128]{2,1,0:T(8,128)(2,1)} %bitcast.4, f32[2048,128]{1,0:T(8,128)} %prior_ref.1, f32[2048,128]{1,0:T(8,128)} %prior_weight_ref.1, ...), custom_call_target="tpu_custom_call" | custom-call | tf_op jit(solution)/shard_map/pallas_call | solution.py:558
  78.7 2.3 %copy.11 = bf16[2,16,128,128]{3,2,1,0:T(8,128)(2,1)} copy(bf16[2,16,128,128]{3,2,1,0:T(8,128)(2,1)} %bitcast.3) | data formatting | bytes 2097152

commit v5 on v4

--- a/solution.py
+++ b/solution.py
@@ -22,12 +22,14 @@
 GROUP = 3 * VIS * TILE
 CH = 32
 CHUNKS = TILE // CH
-GATHERED = 5
 MAIN = NPROF * TILE
 DEEP = MAIN + 3 * TILE
 OWNERS = 16
 VISITORS = 8
 CAP = 4
+GATHERED = 5
+GROUPS = (OWNERS - 1) // GATHERED
+AHEAD = 4
 MESH = pl.DeviceIdType.MESH
 
 
@@ -327,13 +329,21 @@
         coef_copy(k, peer(k), me).start()
         label_copy(k, peer(k), me).start()
 
+    def send_tiles(batch):
+        part = batch // GROUPS
+
+        @pl.loop(1, GATHERED + 1)
+        def _(n):
+            k = (batch % GROUPS) * GATHERED + n
+            pack(part, peer(k), outgoing_ref, peer(k))
+            tile_copy(part, k, peer(k), me).start()
+
+    @pl.loop(0, AHEAD)
+    def _(batch):
+        send_tiles(batch)
+
     @pl.loop(0, CHUNKS)
     def _(part):
-        @pl.loop(1, OWNERS)
-        def _(k):
-            pack(part, peer(k), outgoing_ref, peer(k))
-            tile_copy(part, k, peer(k), me).start()
-
         pack(part, me, arrived_ref, me)
 
     labels_vmem[me] = label_out[...]
@@ -378,6 +388,11 @@
         @pl.loop(0, (OWNERS - 1) // GATHERED)
         def _(group):
             arrive(arrived_ref.at[part, pl.ds(0, GATHERED)], tile_recv.at[part, group])
+            batch = part * GROUPS + group + AHEAD
+
+            @pl.when(batch < CHUNKS * GROUPS)
+            def _():
+                send_tiles(batch)
 
             @pl.loop(1, GATHERED + 1)
             def _(k):

time: 82.1 us -> 80.8 us (0.984)
  Pallas kernels: 78.7 us -> 77.7 us
    pallas_call x1, Pallas kernels: 78.7 us -> 77.7 us  [body(): pl.pallas_call(kernel, out_shape=jax.ShapeDtypeStruct((slots, TILE, TILE)...]
where the time goes in v5:
time: 80.8 us; the launch traced here: 80 us
  Pallas kernels  77.7 us (96%)
  local copies, waits for them, and re-layouts  2.31 us (3%)
    pallas_call x1, Pallas kernels, body(): pl.pallas_call(kernel, out_shape=jax.ShapeDtypeStruct((slots, TILE, TILE)...  77.7 us
    unnamed x1, local copies, waits for them, and re-layouts  2.31 us

profile of v5, /device:TPU:0, one launch (start us, length us, event | category | flops | bytes accessed | tf_op | source)
XLA Modules:
  0.0 80.0 jit_solution(1517292755157004303)
XLA Ops:
  0.0 77.7 %shard_map.91 = bf16[32,128,128]{2,1,0:T(8,128)(2,1)} custom-call(s32[2,16]{1,0:T(2,128)} %ids_ref.1, s32[2,16]{1,0:T(2,128)} %valid_ref.1, bf16[2,16]{1,0:T(2,128)(2,1)} %weights_ref.1, bf16[6,2,25]{2,1,0:T(2,128)(2,1)} %bitcast.5, bf16[32,128,128]{2,1,0:T(8,128)(2,1)} %bitcast.4, f32[2048,128]{1,0:T(8,128)} %prior_ref.1, f32[2048,128]{1,0:T(8,128)} %prior_weight_ref.1, ...), custom_call_target="tpu_custom_call" | custom-call | tf_op jit(solution)/shard_map/pallas_call | solution.py:573
  77.7 2.3 %copy.11 = bf16[2,16,128,128]{3,2,1,0:T(8,128)(2,1)} copy(bf16[2,16,128,128]{3,2,1,0:T(8,128)(2,1)} %bitcast.3) | data formatting | bytes 2097152

commit v6 on v5

--- a/solution.py
+++ b/solution.py
@@ -27,9 +27,9 @@
 OWNERS = 16
 VISITORS = 8
 CAP = 4
-GATHERED = 5
+GATHERED = 3
 GROUPS = (OWNERS - 1) // GATHERED
-AHEAD = 4
+AHEAD = 7
 MESH = pl.DeviceIdType.MESH
 
 

time: 80.8 us -> 80.5 us (level)
  no operation moved by 1% of the time
where the time goes in v6:
time: 80.5 us; the launch traced here: 79.7 us
  Pallas kernels  77.4 us (96%)
  local copies, waits for them, and re-layouts  2.31 us (3%)
    pallas_call x1, Pallas kernels, body(): pl.pallas_call(kernel, out_shape=jax.ShapeDtypeStruct((slots, TILE, TILE)...  77.4 us
    unnamed x1, local copies, waits for them, and re-layouts  2.31 us

profile of v6, /device:TPU:0, one launch (start us, length us, event | category | flops | bytes accessed | tf_op | source)
XLA Modules:
  0.0 79.7 jit_solution(17873603842178574348)
XLA Ops:
  0.0 77.4 %shard_map.91 = bf16[32,128,128]{2,1,0:T(8,128)(2,1)} custom-call(s32[2,16]{1,0:T(2,128)} %ids_ref.1, s32[2,16]{1,0:T(2,128)} %valid_ref.1, bf16[2,16]{1,0:T(2,128)(2,1)} %weights_ref.1, bf16[6,2,25]{2,1,0:T(2,128)(2,1)} %bitcast.5, bf16[32,128,128]{2,1,0:T(8,128)(2,1)} %bitcast.4, f32[2048,128]{1,0:T(8,128)} %prior_ref.1, f32[2048,128]{1,0:T(8,128)} %prior_weight_ref.1, ...), custom_call_target="tpu_custom_call" | custom-call | tf_op jit(solution)/shard_map/pallas_call | solution.py:573
  77.4 2.3 %copy.11 = bf16[2,16,128,128]{3,2,1,0:T(8,128)(2,1)} copy(bf16[2,16,128,128]{3,2,1,0:T(8,128)(2,1)} %bitcast.3) | data formatting | bytes 2097152

commit v7 on v6

--- a/solution.py
+++ b/solution.py
@@ -492,11 +492,9 @@
             wait_strips(step - 2)
 
     finish(CHUNKS - 2)
+    wait_strips(CHUNKS - 3)
     gather(CHUNKS - 1)
-
-    @pl.loop(CHUNKS - 3, CHUNKS - 1)
-    def _(part):
-        wait_strips(part)
+    wait_strips(CHUNKS - 2)
 
     @pl.loop(0, CHUNKS)
     def _(step):
@@ -512,21 +510,17 @@
         def _():
             finish(CHUNKS - 1)
 
-        @pl.loop(1, OWNERS)
-        def _(k):
-            to = peer(k)
-            for c in range(CAP):
-                back_out[part, to, c] = matched_ref[labels_ref[to, 0, me * CAP + c]]
-            for q in range(CHUNKS):
-
-                @pl.when(part == q)
-                def _():
-                    back_copy(q, k, to, me).start()
-
         for q in range(CHUNKS):
 
             @pl.when(part == q)
             def _():
+                @pl.loop(1, OWNERS)
+                def _(k):
+                    to = peer(k)
+                    for c in range(CAP):
+                        back_out[q, to, c] = matched_ref[labels_ref[to, 0, me * CAP + c]]
+                    back_copy(q, k, to, me).start()
+
                 for c in range(CAP):
                     returned[q][me, c] = matched_ref[labels_ref[me, 0, me * CAP + c]]
 

time: 80.5 us -> 80.4 us (level)
  no operation moved by 1% of the time
where the time goes in v7:
time: 80.4 us; the launch traced here: 79.7 us
  Pallas kernels  77.4 us (96%)
  local copies, waits for them, and re-layouts  2.31 us (3%)
    pallas_call x1, Pallas kernels, body(): pl.pallas_call(kernel, out_shape=jax.ShapeDtypeStruct((slots, TILE, TILE)...  77.4 us
    unnamed x1, local copies, waits for them, and re-layouts  2.31 us

profile of v7, /device:TPU:0, one launch (start us, length us, event | category | flops | bytes accessed | tf_op | source)
XLA Modules:
  0.0 79.7 jit_solution(10803557373778474354)
XLA Ops:
  0.0 77.4 %shard_map.91 = bf16[32,128,128]{2,1,0:T(8,128)(2,1)} custom-call(s32[2,16]{1,0:T(2,128)} %ids_ref.1, s32[2,16]{1,0:T(2,128)} %valid_ref.1, bf16[2,16]{1,0:T(2,128)(2,1)} %weights_ref.1, bf16[6,2,25]{2,1,0:T(2,128)(2,1)} %bitcast.5, bf16[32,128,128]{2,1,0:T(8,128)(2,1)} %bitcast.4, f32[2048,128]{1,0:T(8,128)} %prior_ref.1, f32[2048,128]{1,0:T(8,128)} %prior_weight_ref.1, ...), custom_call_target="tpu_custom_call" | custom-call | tf_op jit(solution)/shard_map/pallas_call | solution.py:567
  77.4 2.3 %copy.11 = bf16[2,16,128,128]{3,2,1,0:T(8,128)(2,1)} copy(bf16[2,16,128,128]{3,2,1,0:T(8,128)(2,1)} %bitcast.3) | data formatting | bytes 2097152
